TPU v7x, 256 devices: a whole 4x4x8 slice. The times are simulated.
256 devices in a mesh: ctx: 16 (over z, x_lo), ep: 16 (over y, x_hi, core).
Axes of the slice: x: 4 (x_hi: 2, x_lo: 2; x = x_hi * 2 + x_lo), y: 4, z: 8, core: 2. Of those that a mesh axis runs over, the one named last changes fastest.
Arguments:
- queries: bfloat16 [8192, 2048], P('ctx', 'ep'), may hold values from -8 to 8
- keys: bfloat16 [8192, 2048], P('ctx', 'ep'), may hold values from -8 to 8
- values: bfloat16 [8192, 2048], P('ctx', 'ep'), may hold values from -6 to 6
- segments: int32 [8192], replicated, may hold values from 0 to 2, as said below
- residual: bfloat16 [8192, 2048], P(('ctx', 'ep')), may hold values from -6 to 6
- out_weight: bfloat16 [2048, 2048], P('ep'), may hold values from -0.125 to 0.125
- norm_gain: float32 [2048], replicated, may hold values from 0.1 to 1.9
- router: float32 [2048, 64], replicated, may hold values from -0.125 to 0.125
- routes: int32 [8192, 6], P(('ctx', 'ep')), may hold values from 0 to 63, all different within a row; in each aligned block of 32 rows (0 to 31, 32 to 63, ...) at most 6 rows name the same one
- gate_weight: bfloat16 [16, 16, 2048, 352], P('ep', 'ctx'), may hold values from -0.125 to 0.125
- up_weight: bfloat16 [16, 16, 2048, 352], P('ep', 'ctx'), may hold values from -0.125 to 0.125
- down_weight: bfloat16 [16, 16, 352, 2048], P('ep', 'ctx'), may hold values from -0.15625 to 0.15625
Outputs:
- layer_out: bfloat16 [8192, 2048], P(('ctx', 'ep'))
Inputs may be any that keep to these rules, and one draw needn't show every extreme that they name: In each aligned block of 32 rows (the rows of one device), no expert is named by more than 6 routes; each row names 6 different experts. `segments`: segment ids start at 0 and never fall along the window.
All inputs are finite; a program needn't handle non-finite values.
Results may differ from a plain program's by a relative error of at most 0.0075.
Values may be sent and summed in bfloat16 or wider, within the bound.
A program may use at most 128 MiB of HBM per device.

v0:
```python
import jax
import jax.numpy as jnp
from jax import lax
from jax.sharding import PartitionSpec as P

HD = 128


def in_one_piece(arrays, axis, dim, along):
    both = jnp.concatenate(arrays, axis=along)
    whole, at, done = (lax.all_gather(both, axis, axis=dim, tiled=True), 0, [])
    for a in arrays:
        done.append(lax.slice_in_dim(whole, at, at + a.shape[along], axis=along))
        at += a.shape[along]
    return tuple(done)


def body(
    queries,
    keys,
    values,
    segments,
    residual,
    out_weight,
    norm_gain,
    router,
    routes,
    gate_weight,
    up_weight,
    down_weight,
):
    rows_ctx = queries.shape[0]
    width_heads = queries.shape[1]
    heads_dev = width_heads // HD
    model_width = residual.shape[1]
    tok_rows = residual.shape[0]
    n_ctx = lax.axis_size("ctx")
    n_ep = lax.axis_size("ep")
    first = lax.axis_index("ctx") * rows_ctx
    q_pos = first + jnp.arange(rows_ctx, dtype=jnp.int32)
    q_seg = lax.dynamic_slice_in_dim(segments, first, rows_ctx)
    q_heads = queries.reshape(rows_ctx, heads_dev, HD)
    scale = HD ** (-0.5)
    start_state = (
        jnp.full((heads_dev, rows_ctx), -1e30, jnp.float32),
        jnp.zeros((heads_dev, rows_ctx), jnp.float32),
        jnp.zeros((rows_ctx, heads_dev, HD), jnp.float32),
    )
    key_rows, value_rows = in_one_piece((keys, values), "ctx", 0, 1)
    count = key_rows.shape[0]
    width = 512

    def one_block(step, state):
        best, total, acc = state
        offset = step * width
        key_block = lax.dynamic_slice_in_dim(key_rows, offset, width).reshape(width, heads_dev, HD)
        value_block = lax.dynamic_slice_in_dim(value_rows, offset, width).reshape(
            width, heads_dev, HD
        )
        k_pos = offset + jnp.arange(width, dtype=jnp.int32)
        k_seg = lax.dynamic_slice_in_dim(segments, offset, width)
        allowed = (q_seg[:, None] == k_seg[None, :]) & (k_pos[None, :] <= q_pos[:, None])
        scores = (
            jnp.einsum("qhd,khd->hqk", q_heads, key_block, preferred_element_type=jnp.float32)
            * scale
        )
        scores = jnp.where(allowed[None], scores, jnp.float32(-1e30))
        new_best = jnp.maximum(best, jnp.max(scores, axis=2))
        factor = jnp.exp(best - new_best)
        expo = jnp.where(allowed[None], jnp.exp(scores - new_best[:, :, None]), jnp.float32(0.0))
        total = total * factor + jnp.sum(expo, axis=2)
        update = jnp.einsum(
            "hqk,khd->qhd",
            expo.astype(jnp.bfloat16),
            value_block,
            preferred_element_type=jnp.float32,
        )
        acc = acc * factor.T[:, :, None] + update
        return (new_best, total, acc)

    best, total, acc = lax.fori_loop(0, count // width, one_block, start_state)
    attended = (acc / total.T[:, :, None]).reshape(rows_ctx, width_heads).astype(jnp.bfloat16)
    all_heads = lax.all_to_all(attended, "ep", split_axis=0, concat_axis=1, tiled=True)
    attn = jnp.dot(
        all_heads,
        lax.all_gather(out_weight, "ep", axis=0, tiled=True),
        preferred_element_type=jnp.float32,
    )
    stream = residual.astype(jnp.float32) + attn
    normed = (
        stream * lax.rsqrt(jnp.mean(stream * stream, axis=1, keepdims=True) + 1e-06) * norm_gain
    ).astype(jnp.bfloat16)
    logits = jnp.dot(normed.astype(jnp.float32), router)
    gates = jax.nn.sigmoid(jnp.take_along_axis(logits, routes, axis=1))
    weights = gates / jnp.sum(gates, axis=1, keepdims=True)
    experts = router.shape[1]
    top_count = routes.shape[1]
    capacity = min(tok_rows, max(2, 2 * tok_rows * top_count // experts))
    exp_ep = experts // n_ep
    slices = n_ctx // exp_ep
    flat = routes.reshape(-1)
    onehot = (flat[:, None] == jnp.arange(experts, dtype=jnp.int32)[None, :]).astype(jnp.int32)
    rank = jnp.sum((jnp.cumsum(onehot, axis=0) - onehot) * onehot, axis=1)
    slot = (flat * capacity + rank).reshape(tok_rows, top_count)
    placed = slot[:, :, None] == jnp.arange(experts * capacity, dtype=jnp.int32)[None, None, :]
    send_table = jnp.any(placed, axis=1).astype(jnp.bfloat16)
    combine = jnp.sum(jnp.where(placed, weights[:, :, None], jnp.float32(0.0)), axis=1)
    buffer = jnp.einsum("tp,td->pd", send_table, normed, preferred_element_type=jnp.float32).astype(
        jnp.bfloat16
    )
    grid = buffer.reshape(n_ep, exp_ep, capacity, model_width)
    gate_local = gate_weight.reshape(model_width, -1)
    up_local = up_weight.reshape(model_width, -1)
    down_local = down_weight.reshape(-1, model_width)
    owned = lax.all_to_all(grid, "ep", split_axis=0, concat_axis=0, tiled=True)
    copies = jnp.repeat(jnp.swapaxes(owned, 0, 1), slices, axis=0)
    arrived = lax.all_to_all(copies, "ctx", split_axis=0, concat_axis=0, tiled=True)
    rows = arrived.reshape(-1, model_width)
    gate = jnp.dot(rows, gate_local, preferred_element_type=jnp.float32)
    upper = jnp.dot(rows, up_local, preferred_element_type=jnp.float32)
    act = (jax.nn.silu(gate) * upper).astype(jnp.bfloat16)
    partial_value = (
        jnp.dot(act, down_local, preferred_element_type=jnp.float32)
        .astype(jnp.bfloat16)
        .reshape(arrived.shape)
    )
    returned = lax.all_to_all(partial_value, "ctx", split_axis=0, concat_axis=0, tiled=True)
    summed = jnp.sum(
        returned.reshape(exp_ep, slices, n_ep, capacity, model_width).astype(jnp.float32), axis=1
    ).astype(jnp.bfloat16)
    back = lax.all_to_all(jnp.swapaxes(summed, 0, 1), "ep", split_axis=0, concat_axis=0, tiled=True)
    expert_rows = back.reshape(-1, model_width)
    mixed = jnp.dot(combine, expert_rows.astype(jnp.float32))
    return (stream + mixed).astype(jnp.bfloat16)


def solution(mesh):
    placed = (
        P("ctx", "ep"),
        P("ctx", "ep"),
        P("ctx", "ep"),
        P(),
        P(("ctx", "ep"), None),
        P("ep", None),
        P(),
        P(),
        P(("ctx", "ep"), None),
        P("ep", "ctx", None, None),
        P("ep", "ctx", None, None),
        P("ep", "ctx", None, None),
    )
    return jax.shard_map(
        body, mesh=mesh, in_specs=placed, out_specs=P(("ctx", "ep"), None), check_vma=False
    )
```

profile of v0, /device:TPU:1, one launch (start us, length us, event | category | flops | bytes accessed | tf_op | source)
XLA Modules:
  0.0 624.5 jit_solution(15981866342729058016)
XLA Ops:
  6.5 1.8 pad_maximum_fusion
  12.0 98.1 %all-gather.3.cloned.1.call-done = bf16[8192,256]{1,0:T(8,128)(2,1)} async-done(((bf16[512,256]{1,0:T(8,128)(2,1)}), bf16[8192,256]{1,0:T(8,128)(2,1)}) %all-gather.3.cloned.1.call-update) | async-done | bytes 4194320 | tf_op jit(solution)/shard_map/all_gather | solution.py:11
  110.1 4.5 fusion.39
  114.5 61.7 %while.18 = (s32[]{:T(128)}, f32[1,512]{1,0:T(1,128)S(1)}, f32[1,512]{1,0:T(1,128)S(1)}, f32[512,1,128]{0,2,1:T(8,128)S(1)}, s32[512]{0:T(512)S(1)}, /*index=5*/...) while((s32[]{:T(128)}, f32[1,512]{1,0:T(1,128)S(1)}, ...), condition=%wide.region_3.4_spmd.clone, body=%wide.region_0.3_spmd.clone.sunk | while | flops 139136512 | bytes 4128979 | solution.py:81
  177.2 8.9 %all-to-all-start = ((bf16[16,32,128]{2,1,0:T(8,128)(2,1)}), bf16[16,32,128]{2,1,0:T(8,128)(2,1)S(1)}, u32[]{:S(2)}, u32[]{:S(2)}) async-start(bf16[16,32,128]{2,1,0:T(8,128)(2,1)} %bitcast.2), calls=%async_computation | async-start | bytes 262144 | tf_op jit(solution)/shard_map/all_to_all | solution.py:83
  186.2 7.5 %all-to-all-done = bf16[16,32,128]{2,1,0:T(8,128)(2,1)S(1)} async-done(((bf16[16,32,128]{2,1,0:T(8,128)(2,1)}), bf16[16,32,128]{2,1,0:T(8,128)(2,1)S(1)}, u32[]{:S(2)}, u32[]{:S(2)}) %all-to-all-start) | async-done | bytes 131104 | tf_op jit(solution)/shard_map/all_to_all | solution.py:83
  194.1 5.0 multiply_reduce_fusion
  199.8 1.8 convolution_convert_fusion.1
  201.6 2.5 reshape.145
  205.5 25.3 %all_to_all.36 = bf16[16,4,6,2048]{3,1,2,0:T(4,128)(2,1)S(1)} all-to-all(bf16[16,4,6,2048]{3,1,2,0:T(4,128)(2,1)S(1)} %copy.68), channel_id=1, replica_groups=mesh['ctx'=16,'ep'=16] {'ep'}, dimensions={0} | all-to-all | bytes 3145728 | tf_op jit(solution)/shard_map/all_to_all | solution.py:115
  232.5 146.2 %all_to_all.37 = bf16[16,16,6,2048]{3,1,2,0:T(8,128)(2,1)S(1)} all-to-all(bf16[16,16,6,2048]{3,1,2,0:T(8,128)(2,1)S(1)} %bitcast.84), channel_id=1, replica_groups=mesh['ctx'=16,'ep'=16] {'ctx'}, dimensions={0} | all-to-all | bytes 12582912 | tf_op jit(solution)/shard_map/all_to_all | solution.py:117
  378.6 7.6 %copy.70 = bf16[16,16,6,2048]{3,2,1,0:T(8,128)(2,1)} copy(bf16[16,16,6,2048]{3,1,2,0:T(8,128)(2,1)S(1)} %all_to_all.37) | data formatting | bytes 12582912 | tf_op jit(solution)/shard_map/all_to_all | solution.py:117
  386.3 11.2 %reshape.147 = bf16[1536,2048]{1,0:T(8,128)(2,1)} reshape(bf16[16,16,6,2048]{3,2,1,0:T(8,128)(2,1)} %copy.70) | data formatting | bytes 12582912 | tf_op jit(solution)/shard_map/reshape | solution.py:118
  397.4 6.6 %fusion.27 = f32[1536,352]{0,1:T(8,128)} fusion(bf16[1536,2048]{1,0:T(8,128)(2,1)} %reshape.147, bf16[1,1,2048,352]{2,3,1,0:T(8,128)(2,1)S(1)} %copy-done.10), kind=kOutput, calls=%fused_computation.42 | convolution fusion | flops 2214592512 | bytes 9895936 | tf_op jit(solution)/shard_map/dot_general | solution.py:119
  404.0 11.8 %convolution_convert_fusion = bf16[1536,2048]{1,0:T(8,128)(2,1)} fusion(bf16[1,1,352,2048]{3,2,1,0:T(8,128)(2,1)S(1)} %copy-done, bf16[1536,2048]{1,0:T(8,128)(2,1)} %reshape.147, f32[1536,352]{0,1:T(8,128)} %fusion.27, bf16[1,1,2048,352]{2,3,1,0:T(8,128)(2,1)} %param.24), kind=kOutput, calls=%fused_computation.32 | convolution fusion | flops 4435574784 | bytes 17629184 | tf_op jit(solution)/shard_map/dot_general | solution.py:123
  415.8 10.9 %reshape.151 = bf16[16,16,6,2048]{3,2,1,0:T(8,128)(2,1)} reshape(bf16[1536,2048]{1,0:T(8,128)(2,1)} %convolution_convert_fusion) | data formatting | bytes 12582912 | tf_op jit(solution)/shard_map/reshape | solution.py:125
  426.7 7.5 %copy.71 = bf16[16,16,6,2048]{3,1,2,0:T(8,128)(2,1)S(1)} copy(bf16[16,16,6,2048]{3,2,1,0:T(8,128)(2,1)} %reshape.151) | data formatting | bytes 12582912 | tf_op jit(solution)/shard_map/reshape | solution.py:125
  434.2 143.1 %all_to_all.38 = bf16[16,16,6,2048]{3,1,2,0:T(8,128)(2,1)S(1)} all-to-all(bf16[16,16,6,2048]{3,1,2,0:T(8,128)(2,1)S(1)} %copy.71), channel_id=1, replica_groups=mesh['ctx'=16,'ep'=16] {'ctx'}, dimensions={0} | all-to-all | bytes 12582912 | tf_op jit(solution)/shard_map/all_to_all | solution.py:127
  578.7 2.4 copy.73
  581.0 7.1 %all-to-all-start.4 = ((bf16[16,4,6,2048]{3,1,2,0:T(4,128)(2,1)}), bf16[16,4,6,2048]{3,1,2,0:T(4,128)(2,1)}, u32[]{:S(2)}, u32[]{:S(2)}) async-start(bf16[16,4,6,2048]{3,1,2,0:T(4,128)(2,1)} %copy.73), calls=%async_computation.4 | async-start | bytes 3145728 | tf_op jit(solution)/shard_map/all_to_all | solution.py:131
  588.7 1.6 gather_fusion
  591.3 19.9 %all-to-all-done.4 = bf16[16,4,6,2048]{3,1,2,0:T(4,128)(2,1)} async-done(((bf16[16,4,6,2048]{3,1,2,0:T(4,128)(2,1)}), bf16[16,4,6,2048]{3,1,2,0:T(4,128)(2,1)}, u32[]{:S(2)}, u32[]{:S(2)}) %all-to-all-start.4) | async-done | bytes 1572896 | tf_op jit(solution)/shard_map/all_to_all | solution.py:131
  611.1 2.6 copy.74
  615.2 2.5 fusion.24
  (192 shorter events, 73.7 us)
Async XLA Ops:
  6.5 397.5 %copy-start = (bf16[1,1,352,2048]{3,2,1,0:T(8,128)(2,1)S(1)}, bf16[1,1,352,2048]{3,2,1,0:T(8,128)(2,1)}, u32[]{:S(2)}) copy-start(bf16[1,1,352,2048]{3,2,1,0:T(8,128)(2,1)} %param.25) | copy-start | bytes 4325380
  6.5 103.6 %all-gather.3.cloned.1.call-start = ((), (), s32[]{:S(2)}) async-start(), calls=%async_computation.5 | async-start | bytes 4456448 | tf_op jit(solution)/shard_map/all_gather | solution.py:11
  8.4 185.7 %all-gather.5.cloned.1.call-start = ((), (), s32[]{:S(2)}) async-start(), calls=%async_computation.6 | async-start | bytes 8912896 | tf_op jit(solution)/shard_map/all_gather | solution.py:86
  12.0 102.5 %copy-start.11 = (bf16[512,128]{1,0:T(8,128)(2,1)S(1)}, bf16[512,128]{1,0:T(8,128)(2,1)}, u32[]{:S(2)}) copy-start(bf16[512,128]{1,0:T(8,128)(2,1)} %param.14) | copy-start | bytes 393220
  114.5 71.5 %copy-start.6 = (s32[32,6]{0,1:T(8,128)S(1)}, s32[32,6]{0,1:T(8,128)}, u32[]{:S(2)}) copy-start(s32[32,6]{0,1:T(8,128)} %param.22) | copy-start | bytes 2308
  114.5 79.6 %copy-start.5 = (bf16[32,2048]{1,0:T(8,128)(2,1)S(1)}, bf16[32,2048]{1,0:T(8,128)(2,1)}, u32[]{:S(2)}) copy-start(bf16[32,2048]{1,0:T(8,128)(2,1)} %param.18) | copy-start | bytes 393220
  177.2 16.5 %all-to-all-start = ((bf16[16,32,128]{2,1,0:T(8,128)(2,1)}), bf16[16,32,128]{2,1,0:T(8,128)(2,1)S(1)}, u32[]{:S(2)}, u32[]{:S(2)}) async-start(bf16[16,32,128]{2,1,0:T(8,128)(2,1)} %bitcast.2), calls=%async_computation | async-start | bytes 262144 | tf_op jit(solution)/shard_map/all_to_all | solution.py:83
  186.2 13.7 %copy-start.7 = (f32[2048]{0:T(1024)S(1)}, f32[2048]{0:T(1024)}, u32[]{:S(2)}) copy-start(f32[2048]{0:T(1024)} %param.20) | copy-start | bytes 24580
  199.1 0.7 copy-start.2
  199.2 0.7 copy-start.8
  386.3 11.2 %copy-start.10 = (bf16[1,1,2048,352]{2,3,1,0:T(8,128)(2,1)S(1)}, bf16[1,1,2048,352]{2,3,1,0:T(8,128)(2,1)}, u32[]{:S(2)}) copy-start(bf16[1,1,2048,352]{2,3,1,0:T(8,128)(2,1)} %param.23) | copy-start | bytes 4325380
  581.0 7.4 %copy-start.3 = (f32[32,2048]{1,0:T(8,128)S(1)}, f32[32,2048]{1,0:T(8,128)}, u32[]{:S(2)}) copy-start(f32[32,2048]{1,0:T(8,128)} %copy-done.2) | copy-start | bytes 786436
  581.0 7.4 %copy-start.4 = (f32[2048,64]{0,1:T(8,128)S(1)}, f32[2048,64]{0,1:T(8,128)}, u32[]{:S(2)}) copy-start(f32[2048,64]{0,1:T(8,128)} %param.21) | copy-start | bytes 1572868
  581.0 7.4 %copy-start.9 = (f32[32]{0:T(128)S(1)}, f32[32]{0:T(128)}, u32[]{:S(2)}) copy-start(f32[32]{0:T(128)} %copy-done.8) | copy-start | bytes 388
  581.0 30.1 %all-to-all-start.4 = ((bf16[16,4,6,2048]{3,1,2,0:T(4,128)(2,1)}), bf16[16,4,6,2048]{3,1,2,0:T(4,128)(2,1)}, u32[]{:S(2)}, u32[]{:S(2)}) async-start(bf16[16,4,6,2048]{3,1,2,0:T(4,128)(2,1)} %copy.73), calls=%async_computation.4 | async-start | bytes 3145728 | tf_op jit(solution)/shard_map/all_to_all | solution.py:131
  611.1 6.6 %copy-start.1 = (bf16[1,1,352,2048]{3,2,1,0:T(8,128)(2,1)S(1)}, bf16[1,1,352,2048]{3,2,1,0:T(8,128)(2,1)}, u32[]{:S(2)}) copy-start(bf16[1,1,352,2048]{3,2,1,0:T(8,128)(2,1)} %param.25) | copy-start | bytes 4325380
Sparse Core Ops, SparseCore 0:
  9.1 100.8 all-gather.2
  112.8 81.2 all-gather.4
where the time goes:
time: 627 us; the launch traced here: 625 us
  blocking collectives  315 us (50%)
  waiting for transfers between devices  127 us (20%)
  local copies, waits for them, and re-layouts  70.8 us (11%)
  matrix products  70.8 us (11%)
  starting transfers between devices  16 us (3%)
  between operations  13.6 us (2%)
  other arithmetic  11.2 us (2%)
    all_to_all x1, blocking collectives, body(): lax.all_to_all(copies, 'ctx', split_axis=0, concat_axis=0, tiled=True)  146 us
    all_to_all x1, blocking collectives, body(): lax.all_to_all(partial_value, 'ctx', split_axis=0, concat_axis=0, tiled=T...  143 us
    all_gather x1, waiting for transfers between devices, in_one_piece(): whole, at, done = (lax.all_gather(both, axis, axis=dim, tiled=True), 0, [])  98.1 us
    all_to_all x1, blocking collectives, body(): owned = lax.all_to_all(grid, 'ep', split_axis=0, concat_axis=0, tiled=True)  25.3 us
    dot_general x16, matrix products, one_block(): jnp.einsum('hqk,khd->qhd', expo.astype(jnp.bfloat16), value_block, prefer...  22.3 us
    dot_general x16, matrix products, one_block(): jnp.einsum('qhd,khd->hqk', q_heads, key_block, preferred_element_type=jnp...  20.6 us
    all_to_all x1, waiting for transfers between devices, body(): lax.all_to_all(jnp.swapaxes(summed, 0, 1), 'ep', split_axis=0, concat_axi...  19.9 us
    reshape x2, local copies, waits for them, and re-layouts, body(): partial_value = jnp.dot(act, down_local, preferred_element_type=jnp.float...  18.5 us
  transfers between devices with their start and end apart: 4, of which 4 were waited for; matrix products, arithmetic and copies ran while one was open for 12% of the time, Pallas kernels for 0%

commit v1 on v0

v1 whole, which is shorter than its diff:
```python
import functools

import jax
import jax.numpy as jnp
from jax import lax
from jax.experimental import pallas as pl
from jax.experimental.pallas import tpu as pltpu
from jax.sharding import PartitionSpec as P

HD = 128
CAP = 6
MESH = pl.DeviceIdType.MESH
ANY = pl.BlockSpec(memory_space=pl.ANY)
BF16 = jnp.bfloat16
F32 = jnp.float32
LOG2E = 1.4426950408889634


def remote(src, dst, send, recv, ctx, ep):
    return pltpu.make_async_remote_copy(
        src_ref=src,
        dst_ref=dst,
        send_sem=send,
        recv_sem=recv,
        device_id=(ctx, ep),
        device_id_type=MESH,
    )


def greet(peers):
    barrier = pltpu.get_barrier_semaphore()
    for ctx, ep in peers:
        pl.semaphore_signal(barrier, inc=1, device_id=(ctx, ep), device_id_type=MESH)
    pl.semaphore_wait(barrier, len(peers))


def params(collective_id, vmem=32 << 20):
    return pltpu.CompilerParams(
        collective_id=collective_id, has_side_effects=True, vmem_limit_bytes=vmem
    )


def gather_kernel(k_ref, v_ref, k_all, v_all, send, recv, local):
    c, e = lax.axis_index("ctx"), lax.axis_index("ep")
    z, x = c // 2, c % 2
    ox = 1 - x
    up, down, side = ((z + 1) % 8) * 2 + x, ((z + 7) % 8) * 2 + x, z * 2 + ox
    greet([(up, e), (down, e), (side, e)])
    own_k = pltpu.make_async_copy(k_ref, k_all.at[c], local.at[0])
    own_v = pltpu.make_async_copy(v_ref, v_all.at[c], local.at[1])
    own_k.start()
    own_v.start()
    started = []
    slots = iter(range(32))

    def go(src, dst, slot, to):
        copy = remote(src, dst, send.at[slot], recv.at[slot], to, e)
        copy.start()
        started.append(copy)
        return copy

    side_k = go(k_ref, k_all.at[c], next(slots), side)
    up_k, down_k, up_v, down_v = {}, {}, {}, {}
    for t in range(1, 5):
        up_k[t] = (next(slots), next(slots))
        down_k[t] = (next(slots), next(slots))
        up_v[t], down_v[t] = next(slots), next(slots)

    copies = {}
    copies["uv", 1] = go(v_ref, v_all.at[c], up_v[1], up)
    copies["dv", 1] = go(v_ref, v_all.at[c], down_v[1], down)
    copies["uk", 1, 0] = go(k_ref, k_all.at[c], up_k[1][0], up)
    copies["dk", 1, 0] = go(k_ref, k_all.at[c], down_k[1][0], down)
    side_v = [go(v_ref, v_all.at[c], next(slots), side)]
    side_k.wait_recv()
    copies["uk", 1, 1] = go(k_all.at[side], k_all.at[side], up_k[1][1], up)
    copies["dk", 1, 1] = go(k_all.at[side], k_all.at[side], down_k[1][1], down)
    extra = iter(range(26, 33))
    for t in range(1, 5):
        below, above = (z + 8 - t) % 8, (z + t) % 8
        if t <= 3:
            copies["uv", t].wait_recv()
            block = v_all.at[below * 2 + x]
            if t <= 2:
                copies["uv", t + 1] = go(block, block, up_v[t + 1], up)
            side_v.append(go(block, block, next(extra), side))
        copies["dv", t].wait_recv()
        block = v_all.at[above * 2 + x]
        if t <= 3:
            copies["dv", t + 1] = go(block, block, down_v[t + 1], down)
        side_v.append(go(block, block, next(extra), side))
        for h, column in ((0, x), (1, ox)):
            copies["uk", t, h].wait_recv()
            block = k_all.at[below * 2 + column]
            if t <= 3:
                copies["uk", t + 1, h] = go(block, block, up_k[t + 1][h], up)
            if t <= 3:
                copies["dk", t, h].wait_recv()
                block = k_all.at[above * 2 + column]
                if t <= 2:
                    copies["dk", t + 1, h] = go(block, block, down_k[t + 1][h], down)
    for copy in side_v:
        copy.wait_recv()
    for copy in started:
        copy.wait_send()
    own_k.wait()
    own_v.wait()


def gather_kv(keys, values):
    out = jax.ShapeDtypeStruct((16,) + keys.shape, BF16)
    return pl.pallas_call(
        gather_kernel,
        out_shape=(out, out),
        in_specs=[ANY, ANY],
        out_specs=(ANY, ANY),
        scratch_shapes=[
            pltpu.SemaphoreType.DMA((34,)),
            pltpu.SemaphoreType.DMA((34,)),
            pltpu.SemaphoreType.DMA((2,)),
        ],
        compiler_params=params(1),
        name="gather_kv",
    )(keys, values)


def attend_kernel(info, q_ref, k_ref, v_ref, qseg_ref, kseg_ref, o_ref, best, total, acc):
    step = pl.program_id(0)
    c, first = info[0], info[1]
    block = c - step
    scale = (HD**-0.5) * LOG2E

    def update(masked, diagonal):
        s = lax.dot_general(
            q_ref[...], k_ref[0], (((1,), (1,)), ((), ())), preferred_element_type=F32
        )
        s = s * scale
        if masked:
            ok = qseg_ref[...] == kseg_ref[0]
            if diagonal:
                rows = lax.broadcasted_iota(jnp.int32, s.shape, 0)
                cols = lax.broadcasted_iota(jnp.int32, s.shape, 1)
                ok = ok & (cols <= rows)
            s = jnp.where(ok, s, -1e30)
        peak = jnp.max(s, axis=1, keepdims=True)
        if diagonal:
            new = peak
            p = jnp.exp2(s - new)
            total[...] = jnp.sum(p, axis=1, keepdims=True)
            acc[...] = jnp.dot(p.astype(BF16), v_ref[0], preferred_element_type=F32)
        else:
            old = best[...]
            new = jnp.maximum(old, peak)
            p = jnp.exp2(s - new)
            factor = jnp.exp2(old - new)
            total[...] = total[...] * factor + jnp.sum(p, axis=1, keepdims=True)
            acc[...] = acc[...] * factor + jnp.dot(
                p.astype(BF16), v_ref[0], preferred_element_type=F32
            )
        best[...] = new

    @pl.when(step == 0)
    def _():
        update(True, True)

    inside = (step > 0) & (block >= first)
    same = block >= info[2]

    @pl.when(inside & same)
    def _():
        update(False, False)

    @pl.when(inside & jnp.logical_not(same))
    def _():
        update(True, False)

    @pl.when(step == pl.num_programs(0) - 1)
    def _():
        o_ref[...] = (acc[...] / total[...]).astype(BF16)


def attend(queries, k_all, v_all, segments):
    rows = queries.shape[0]
    c = lax.axis_index("ctx")
    start = c * rows
    q_seg = lax.dynamic_slice_in_dim(segments, start, rows)
    first = jnp.sum((segments < q_seg[0]).astype(jnp.int32)) // rows
    same = (jnp.sum((segments < q_seg[rows - 1]).astype(jnp.int32)) + rows - 1) // rows
    info = jnp.stack([c, first, same]).astype(jnp.int32)

    def kv(i, info):
        return (jnp.maximum(info[0] - i, info[1]), 0, 0)

    return pl.pallas_call(
        attend_kernel,
        out_shape=jax.ShapeDtypeStruct(queries.shape, BF16),
        grid_spec=pltpu.PrefetchScalarGridSpec(
            num_scalar_prefetch=1,
            grid=(16,),
            in_specs=[
                pl.BlockSpec((rows, HD), lambda i, info: (0, 0)),
                pl.BlockSpec((1, rows, HD), kv),
                pl.BlockSpec((1, rows, HD), kv),
                pl.BlockSpec((rows, 1), lambda i, info: (0, 0)),
                pl.BlockSpec((1, 1, rows), kv),
            ],
            out_specs=pl.BlockSpec((rows, HD), lambda i, info: (0, 0)),
            scratch_shapes=[
                pltpu.VMEM((rows, 1), F32),
                pltpu.VMEM((rows, 1), F32),
                pltpu.VMEM((rows, HD), F32),
            ],
        ),
        compiler_params=pltpu.CompilerParams(vmem_limit_bytes=32 << 20),
        name="attend",
    )(info, queries, k_all, v_all, q_seg.reshape(rows, 1), segments.reshape(16, 1, rows))


def heads_kernel(a_ref, r_ref, a_out, r_out, send, recv, rsend, rrecv, local):
    c, e = lax.axis_index("ctx"), lax.axis_index("ep")
    core, m = e % 2, e // 2
    greet([(c, (e + d) % 16) for d in range(1, 16)])
    own_a = pltpu.make_async_copy(a_ref.at[e], a_out.at[e], local.at[0])
    own_r = pltpu.make_async_copy(r_ref, r_out.at[m], local.at[1])
    own_a.start()
    own_r.start()
    copies = []
    for d in range(1, 16):
        to = (e + d) % 16
        copies.append(remote(a_ref.at[to], a_out.at[e], send.at[d], recv.at[d], c, to))
        copies[-1].start()
    for d in range(1, 8):
        to = ((m + d) % 8) * 2 + core
        copies.append(remote(r_ref, r_out.at[m], rsend.at[d], rrecv.at[d], c, to))
        copies[-1].start()
    for copy in copies:
        copy.wait()
    own_a.wait()
    own_r.wait()


def exchange_heads(attended, routes):
    return pl.pallas_call(
        heads_kernel,
        out_shape=(
            jax.ShapeDtypeStruct(attended.shape, BF16),
            jax.ShapeDtypeStruct((8,) + routes.shape, jnp.int32),
        ),
        in_specs=[ANY, ANY],
        out_specs=(ANY, ANY),
        scratch_shapes=[
            pltpu.SemaphoreType.DMA((16,)),
            pltpu.SemaphoreType.DMA((16,)),
            pltpu.SemaphoreType.DMA((8,)),
            pltpu.SemaphoreType.DMA((8,)),
            pltpu.SemaphoreType.DMA((2,)),
        ],
        compiler_params=params(2),
        name="exchange_heads",
    )(attended, routes)


def group_kernel(scatter, a_ref, a_out, send, recv, local):
    c, e = lax.axis_index("ctx"), lax.axis_index("ep")
    core, m = e % 2, e // 2
    greet([(c, ((m + d) % 8) * 2 + core) for d in range(1, 8)])
    own = pltpu.make_async_copy(a_ref.at[m] if scatter else a_ref, a_out.at[m], local)
    own.start()
    copies = []
    for d in range(1, 8):
        to = (m + d) % 8
        src = a_ref.at[to] if scatter else a_ref
        copies.append(remote(src, a_out.at[m], send.at[d], recv.at[d], c, to * 2 + core))
        copies[-1].start()
    for copy in copies:
        copy.wait()
    own.wait()


def group_exchange(rows, scatter, collective_id):
    shape = rows.shape[-2:]
    return pl.pallas_call(
        functools.partial(group_kernel, scatter),
        out_shape=jax.ShapeDtypeStruct((8,) + shape, rows.dtype),
        in_specs=[ANY],
        out_specs=ANY,
        scratch_shapes=[
            pltpu.SemaphoreType.DMA((8,)),
            pltpu.SemaphoreType.DMA((8,)),
            pltpu.SemaphoreType.DMA,
        ],
        compiler_params=params(collective_id),
        name="group_scatter" if scatter else "group_gather",
    )(rows)


def project_kernel(a_ref, w_ref, res_ref, gain_ref, stream_ref, normed_ref, acc):
    step = pl.program_id(0)

    @pl.when(step == 0)
    def _():
        acc[...] = res_ref[...].astype(F32)

    part = jnp.dot(a_ref[0], w_ref[0:HD, :], preferred_element_type=F32)
    for h in range(1, a_ref.shape[0]):
        part += jnp.dot(
            a_ref[h], w_ref[h * HD : (h + 1) * HD, :], preferred_element_type=F32
        )
    acc[...] += part

    @pl.when(step == pl.num_programs(0) - 1)
    def _():
        s = acc[...]
        stream_ref[...] = s
        mean = jnp.mean(s * s, axis=1, keepdims=True)
        normed_ref[...] = (s * lax.rsqrt(mean + 1e-06) * gain_ref[...]).astype(BF16)


def project(heads, weight, residual, gain):
    tok, width = residual.shape
    n = heads.shape[0]
    per = 2
    return pl.pallas_call(
        project_kernel,
        out_shape=(
            jax.ShapeDtypeStruct((tok, width), F32),
            jax.ShapeDtypeStruct((tok, width), BF16),
        ),
        grid=(n // per,),
        in_specs=[
            pl.BlockSpec((per, tok, HD), lambda i: (i, 0, 0)),
            pl.BlockSpec((per * HD, width), lambda i: (i, 0)),
            pl.BlockSpec((tok, width), lambda i: (0, 0)),
            pl.BlockSpec((1, width), lambda i: (0, 0)),
        ],
        out_specs=(
            pl.BlockSpec((tok, width), lambda i: (0, 0)),
            pl.BlockSpec((tok, width), lambda i: (0, 0)),
        ),
        scratch_shapes=[pltpu.VMEM((tok, width), F32)],
        compiler_params=pltpu.CompilerParams(vmem_limit_bytes=32 << 20),
        name="project",
    )(heads, weight, residual, gain.reshape(1, width))


def dispatch_kernel(tok_ref, route_ref, router_ref, column_ref, rows_ref, weight_ref):
    count = tok_ref.shape[0]
    experts = router_ref.shape[1]
    width = column_ref.shape[1]
    routes = route_ref[...]
    ids = lax.broadcasted_iota(jnp.int32, (count, experts), 1)
    named = routes[:, 0:1] == ids
    for k in range(1, 6):
        named = named | (routes[:, k : k + 1] == ids)
    named = named.astype(F32)
    t0 = lax.broadcasted_iota(jnp.int32, (count, count), 0)
    t1 = lax.broadcasted_iota(jnp.int32, (count, count), 1)
    before = ((t1 < t0) & (t1 // 32 == t0 // 32)).astype(BF16)
    rank = jnp.dot(before, named.astype(BF16), preferred_element_type=F32)
    owner = lax.broadcasted_iota(jnp.int32, (count, experts), 0) // 32
    place = jnp.where(named > 0, rank + (owner * CAP).astype(F32), -1.0)
    expert_of = column_ref[0:1, :]
    slot_of = column_ref[1:2, :].astype(F32)
    pick = (
        lax.broadcasted_iota(jnp.int32, (experts, width), 0) == expert_of
    ).astype(BF16)
    spread = jnp.dot(place.astype(BF16), pick, preferred_element_type=F32)
    chosen = spread == slot_of
    rows_ref[...] = lax.dot_general(
        chosen.astype(BF16),
        tok_ref[...],
        (((0,), (0,)), ((), ())),
        preferred_element_type=F32,
    ).astype(BF16)
    router = router_ref[...]
    high = router.astype(BF16)
    low = (router - high.astype(F32)).astype(BF16)
    tokens = tok_ref[...]
    logits = jnp.dot(tokens, high, preferred_element_type=F32) + jnp.dot(
        tokens, low, preferred_element_type=F32
    )
    gates = named * jax.nn.sigmoid(logits)
    weights = gates / jnp.sum(gates, axis=1, keepdims=True)
    high = weights.astype(BF16)
    low = (weights - high.astype(F32)).astype(BF16)
    spread = jnp.dot(high, pick, preferred_element_type=F32) + jnp.dot(
        low, pick, preferred_element_type=F32
    )
    weight_ref[...] = jnp.where(chosen, spread, 0.0)


def dispatch(tokens, routes, router, columns):
    count, width = tokens.shape
    n = columns.shape[1]
    return pl.pallas_call(
        dispatch_kernel,
        out_shape=(
            jax.ShapeDtypeStruct((n, width), BF16),
            jax.ShapeDtypeStruct((count, n), F32),
        ),
        compiler_params=pltpu.CompilerParams(vmem_limit_bytes=32 << 20),
        name="dispatch",
    )(tokens, routes, router, columns)


def combine_kernel(weight_ref, rows_ref, out_ref):
    weights = weight_ref[...]
    high = weights.astype(BF16)
    low = (weights - high.astype(F32)).astype(BF16)
    rows = rows_ref[...]
    out_ref[...] = (
        jnp.dot(high, rows, preferred_element_type=F32)
        + jnp.dot(low, rows, preferred_element_type=F32)
    ).astype(BF16)


def combine(weights, rows):
    return pl.pallas_call(
        combine_kernel,
        out_shape=jax.ShapeDtypeStruct((weights.shape[0], rows.shape[1]), BF16),
        compiler_params=pltpu.CompilerParams(vmem_limit_bytes=32 << 20),
        name="combine",
    )(weights, rows)


def final_kernel(stream_ref, part_ref, out_ref):
    total = stream_ref[...]
    for m in range(8):
        total = total + part_ref[m].astype(F32)
    out_ref[...] = total.astype(BF16)


def finish(stream, parts):
    return pl.pallas_call(
        final_kernel,
        out_shape=jax.ShapeDtypeStruct(stream.shape, BF16),
        compiler_params=pltpu.CompilerParams(vmem_limit_bytes=32 << 20),
        name="finish",
    )(stream, parts)


def away(i):
    half = (i + 1) // 2
    return half * (2 * (i % 2) - 1)


def expert_kernel(
    rows_ref,
    wg_ref,
    wu_ref,
    wd_ref,
    back_ref,
    xs,
    ps,
    from_core,
    from_side,
    sums,
    done,
    wg,
    wu,
    wd,
    z_send,
    z_recv,
    x_send,
    x_recv,
    s_send,
    s_recv,
    c_send,
    c_recv,
    f_send,
    f_recv,
    b_send,
    b_recv,
    local,
):
    c, e = lax.axis_index("ctx"), lax.axis_index("ep")
    z, x = c // 2, c % 2
    side, other = z * 2 + (1 - x), e + 1 - 2 * (e % 2)
    n = 8
    loads = [
        pltpu.make_async_copy(wg_ref, wg, local.at[0]),
        pltpu.make_async_copy(wu_ref, wu, local.at[1]),
        pltpu.make_async_copy(wd_ref, wd, local.at[2]),
    ]
    for load in loads:
        load.start()
    own = pltpu.make_async_copy(rows_ref.at[0], xs.at[0, 0], local.at[3])
    own.start()
    peers = [(((z + d) % n) * 2 + x, e) for d in range(1, n)]
    greet(peers + [(side, e), (c, other)])

    def out(i):
        to = ((z + n - away(i)) % n) * 2 + x
        return remote(rows_ref.at[i], xs.at[i, 0], z_send.at[i], z_recv.at[i], to, e)

    def to_side(i):
        return remote(xs.at[i, 0], xs.at[i, 1], x_send.at[i], x_recv.at[i], side, e)

    def to_core(i, q):
        return remote(
            xs.at[i, q], xs.at[i, q + 2], s_send.at[i, q], s_recv.at[i, q], c, other
        )

    def sum_core(i):
        return remote(
            ps.at[i, pl.ds(2, 2)], from_core.at[i], c_send.at[i], c_recv.at[i], c, other
        )

    def sum_side(i):
        return remote(
            sums.at[i], from_side.at[i], f_send.at[i], f_recv.at[i], side, e
        )

    def home(i):
        to = ((z + n + away(i)) % n) * 2 + x
        return remote(done.at[i], back_ref.at[i], b_send.at[i], b_recv.at[i], to, e)

    for i in range(1, n):
        out(i).start()
    own.wait()
    for load in loads:
        load.wait()

    def step(s, carry):
        @pl.when(s < n)
        def _():
            @pl.when(s > 0)
            def _():
                out(s).wait_recv()

            to_side(s).start()
            to_core(s, 0).start()

        @pl.when((s >= 1) & (s < n + 1))
        def _():
            i = s - 1
            to_side(i).wait_recv()
            to_core(i, 1).start()

        @pl.when((s >= 2) & (s < n + 2))
        def _():
            i = s - 2
            to_core(i, 0).wait_recv()
            to_core(i, 1).wait_recv()
            shape = xs.shape[1:]
            rows = xs[i].reshape(shape[0] * shape[1], shape[2])
            gate = jnp.dot(rows, wg[...], preferred_element_type=F32)
            upper = jnp.dot(rows, wu[...], preferred_element_type=F32)
            act = (gate / (1.0 + jnp.exp(-gate)) * upper).astype(BF16)
            part = jnp.dot(act, wd[...], preferred_element_type=F32)
            ps[i] = part.astype(BF16).reshape(shape)
            sum_core(i).start()

        @pl.when((s >= 3) & (s < n + 3))
        def _():
            i = s - 3
            sum_core(i).wait_recv()
            sums[i] = (ps[i, 1].astype(F32) + from_core[i, 1].astype(F32)).astype(BF16)
            sum_side(i).start()

        @pl.when(s >= 4)
        def _():
            i = s - 4
            sum_side(i).wait_recv()
            done[i] = (
                ps[i, 0].astype(F32) + from_core[i, 0].astype(F32) + from_side[i].astype(F32)
            ).astype(BF16)

            @pl.when(i > 0)
            def _():
                home(i).start()

        return carry

    lax.fori_loop(0, n + 4, step, 0)
    last = pltpu.make_async_copy(done.at[0], back_ref.at[0], local.at[3])
    last.start()

    def drain(i, carry):
        to_side(i).wait_send()
        to_core(i, 0).wait_send()
        to_core(i, 1).wait_send()
        sum_core(i).wait_send()
        sum_side(i).wait_send()

        @pl.when(i > 0)
        def _():
            out(i).wait_send()
            home(i).wait()

        return carry

    lax.fori_loop(0, n, drain, 0)
    last.wait()


def experts(rows, wg, wu, wd):
    n, cap, width = rows.shape
    dma = pltpu.SemaphoreType.DMA
    return pl.pallas_call(
        expert_kernel,
        out_shape=jax.ShapeDtypeStruct(rows.shape, BF16),
        in_specs=[ANY] * 4,
        out_specs=ANY,
        scratch_shapes=[
            pltpu.VMEM((n, 4, cap, width), BF16),
            pltpu.VMEM((n, 4, cap, width), BF16),
            pltpu.VMEM((n, 2, cap, width), BF16),
            pltpu.VMEM((n, cap, width), BF16),
            pltpu.VMEM((n, cap, width), BF16),
            pltpu.VMEM((n, cap, width), BF16),
            pltpu.VMEM(wg.shape, BF16),
            pltpu.VMEM(wu.shape, BF16),
            pltpu.VMEM(wd.shape, BF16),
            dma((n,)),
            dma((n,)),
            dma((n,)),
            dma((n,)),
            dma((n, 2)),
            dma((n, 2)),
            dma((n,)),
            dma((n,)),
            dma((n,)),
            dma((n,)),
            dma((n,)),
            dma((n,)),
            dma((4,)),
        ],
        compiler_params=params(3, 56 << 20),
        name="experts",
    )(rows, wg, wu, wd)


def swap_pairs():
    pairs = []
    for c in range(16):
        for e in range(16):
            move = ((c >> 1) & 1) != (e & 1)
            to = ((c ^ 2) * 16 + (e ^ 1)) if move else c * 16 + e
            pairs.append((c * 16 + e, to))
    return pairs


def body(
    queries,
    keys,
    values,
    segments,
    residual,
    out_weight,
    norm_gain,
    router,
    routes,
    gate_weight,
    up_weight,
    down_weight,
):
    tok, width = residual.shape
    c, e = lax.axis_index("ctx"), lax.axis_index("ep")
    pairs = swap_pairs()
    wg = lax.ppermute(gate_weight[0, 0], ("ctx", "ep"), pairs)
    wu = lax.ppermute(up_weight[0, 0], ("ctx", "ep"), pairs)
    wd = lax.ppermute(down_weight[0, 0], ("ctx", "ep"), pairs)
    weight = lax.all_gather(out_weight, "ep", axis=0, tiled=True)
    k_all, v_all = gather_kv(keys, values)
    attended = attend(queries, k_all, v_all, segments)
    padded = jnp.pad(routes, ((0, 0), (0, 128 - routes.shape[1])), constant_values=-1)
    heads, group_routes = exchange_heads(attended.reshape(16, tok, HD), padded)
    stream, normed = project(heads, weight, residual, norm_gain)
    tokens = group_exchange(normed, False, 4).reshape(8 * tok, width)
    block = jnp.arange(8, dtype=jnp.int32)
    at = (c // 2 + 8 - away(block)) % 8
    expert = 8 * (e // 2) + 4 * (at % 2) + at // 2
    slots = 8 * CAP
    columns = jnp.stack(
        [
            jnp.repeat(expert, slots),
            jnp.tile(jnp.arange(slots, dtype=jnp.int32), 8),
        ]
    ).astype(jnp.int32)
    rows, weights = dispatch(tokens, group_routes.reshape(8 * tok, 128), router, columns)
    back = experts(rows.reshape(8, slots, width), wg, wu, wd)
    mixed = combine(weights, back.reshape(8 * slots, width))
    parts = group_exchange(mixed.reshape(8, tok, width), True, 5)
    return finish(stream, parts)


def solution(mesh):
    placed = (
        P("ctx", "ep"),
        P("ctx", "ep"),
        P("ctx", "ep"),
        P(),
        P(("ctx", "ep"), None),
        P("ep", None),
        P(),
        P(),
        P(("ctx", "ep"), None),
        P("ep", "ctx", None, None),
        P("ep", "ctx", None, None),
        P("ep", "ctx", None, None),
    )
    return jax.shard_map(
        body, mesh=mesh, in_specs=placed, out_specs=P(("ctx", "ep"), None), check_vma=False
    )
```

time: 627 us -> 285 us (0.45)
  blocking collectives: 315 us -> 0 us
  Pallas kernels: 0 us -> 236 us
  waiting for transfers between devices: 127 us -> 0.69 us
  matrix products: 70.8 us -> 0 us
  local copies, waits for them, and re-layouts: 70.8 us -> 14.1 us
  other arithmetic: 11.2 us -> 2.89 us
    all_to_all x3 -> x0, blocking collectives: 315 us -> none  [the longest x1 146 us: body(): lax.all_to_all(copies, 'ctx', split_axis=0, concat_axis=0, tiled=True)]
    pallas_call x0 -> x10, Pallas kernels: none -> 236 us  [the longest x1 106 us: experts(): pl.pallas_call(expert_kernel, out_shape=jax.ShapeDtypeStruct(rows.shape,...]
    all_gather x2 -> x1, waiting for transfers between devices: 98.5 us -> 0.01 us  [body(): weight = lax.all_gather(out_weight, 'ep', axis=0, tiled=True)]
    dot_general x38 -> x0, matrix products: 70.8 us -> none  [the longest x16 22.3 us: one_block(): jnp.einsum('hqk,khd->qhd', expo.astype(jnp.bfloat16), value_block, prefer...]
    reshape x6 -> x1, local copies, waits for them, and re-layouts: 34.9 us -> 0.14 us  [attend(): q_seg.reshape(rows, 1)]
    all_to_all x2 -> x0, waiting for transfers between devices: 27.4 us -> none  [the longest x1 19.9 us: body(): lax.all_to_all(jnp.swapaxes(summed, 0, 1), 'ep', split_axis=0, concat_axi...]
    all_to_all x2 -> x0, starting transfers between devices: 16 us -> none  [the longest x1 8.86 us: body(): lax.all_to_all(attended, 'ep', split_axis=0, concat_axis=1, tiled=True)]
    dynamic_slice x17 -> x1, local copies, waits for them, and re-layouts: 13.1 us -> 0.76 us  [attend(): q_seg = lax.dynamic_slice_in_dim(segments, start, rows)]
  transfers between devices with their start and end apart: 4 -> 4, of which waited for: 4 -> 0; matrix products, arithmetic and copies ran while one was open for 12% -> 4% of each run, Pallas kernels for 0% -> 38%
where the time goes in v1:
time: 285 us; the launch traced here: 281 us
  Pallas kernels  236 us (83%)
  between operations  16.5 us (6%)
  local copies, waits for them, and re-layouts  14.1 us (5%)
  starting transfers between devices  10.5 us (4%)
  other arithmetic  2.89 us (1%)
    pallas_call x1, Pallas kernels, experts(): pl.pallas_call(expert_kernel, out_shape=jax.ShapeDtypeStruct(rows.shape,...  106 us
    pallas_call x1, Pallas kernels, gather_kv(): pl.pallas_call(gather_kernel, out_shape=(out, out), in_specs=[ANY, ANY],...  71.2 us
    pallas_call x2, Pallas kernels, group_exchange(): pl.pallas_call(functools.partial(group_kernel, scatter), out_shape=jax.Sh...  38.9 us
    pallas_call x1, Pallas kernels, exchange_heads(): pl.pallas_call(heads_kernel, out_shape=(jax.ShapeDtypeStruct(attended.sha...  11 us
    unnamed x20, local copies, waits for them, and re-layouts  8.16 us
  transfers between devices with their start and end apart: 4, of which 0 were waited for; matrix products, arithmetic and copies ran while one was open for 4% of the time, Pallas kernels for 38%

profile of v1, /device:TPU:1, one launch (start us, length us, event | category | flops | bytes accessed | tf_op | source)
XLA Modules:
  0.0 280.6 jit_solution(13226098371939815148)
XLA Ops:
  6.6 0.7 all-gather.2.cloned.1.call-update
  7.3 4.9 %collective-permute-start = (bf16[2048,352]{0,1:T(8,128)(2,1)}, bf16[2048,352]{0,1:T(8,128)(2,1)}, u32[]{:S(2)}, u32[]{:S(2)}) collective-permute-start(bf16[2048,352]{0,1:T(8,128)(2,1)} %bitcast.26), channel_id=1, source_target_pairs={{0,0},{1,32},{2,2},{3,34},{4,4},{5,36},{6,6},{7,38},{8,8},{9,40},{... | collective-permute-start | bytes 4325384 | tf_op jit(solution)/shard_map/ppermute | solution.py:661
  12.2 1.9 collective-permute-start.1
  14.1 3.6 %collective-permute-start.2 = (bf16[352,2048]{1,0:T(8,128)(2,1)}, bf16[352,2048]{1,0:T(8,128)(2,1)}, u32[]{:S(2)}, u32[]{:S(2)}) collective-permute-start(bf16[352,2048]{1,0:T(8,128)(2,1)} %bitcast.28), channel_id=1, source_target_pairs={{0,0},{1,32},{2,2},{3,34},{4,4},{5,36},{6,6},{7,38},{8,8},{9,40},{... | collective-permute-start | bytes 4325384 | tf_op jit(solution)/shard_map/ppermute | solution.py:663
  17.8 0.8 dynamic_slice.3
  18.6 0.6 fusion.9
  19.2 2.8 convert_reduce_fusion.1
  25.1 0.8 copy.23
  26.1 1.4 copy.24.router_ref
  27.6 71.2 %gather_kv.1 = (bf16[16,512,128]{2,1,0:T(8,128)(2,1)S(1)}, bf16[16,512,128]{2,1,0:T(8,128)(2,1)S(1)}) custom-call(bf16[512,128]{1,0:T(8,128)(2,1)S(1)} %copy-done.6, bf16[512,128]{1,0:T(8,128)(2,1)S(1)} %copy-done.7), custom_call_target="tpu_custom_call" | custom-call | tf_op jit(solution)/shard_map/gather_kv/pallas_call | solution.py:112
  98.9 2.1 attend.1
  101.0 11.0 %exchange_heads.1 = (bf16[16,32,128]{2,1,0:T(8,128)(2,1)S(1)}, s32[8,32,128]{2,1,0:T(8,128)S(1)}) custom-call(bf16[16,32,128]{2,1,0:T(8,128)(2,1)S(1)} %bitcast.21, s32[32,128]{1,0:T(8,128)S(1)} %pad.4.r_ref), custom_call_target="tpu_custom_call" | custom-call | tf_op jit(solution)/shard_map/exchange_heads/pallas_call | solution.py:243
  112.1 2.6 copy.25.wg_ref
  114.7 1.6 copy.26.wu_ref
  116.3 3.4 %copy-done = bf16[2048,2048]{1,0:T(8,128)(2,1)S(1)} copy-done((bf16[2048,2048]{1,0:T(8,128)(2,1)S(1)}, bf16[2048,2048]{1,0:T(8,128)(2,1)}, u32[]{:S(2)}) %copy-start) | copy-done | bytes 8388632
  119.7 2.4 project.1
  122.1 17.6 %group_gather.1 = bf16[8,32,2048]{2,1,0:T(8,128)(2,1)S(1)} custom-call(bf16[32,2048]{1,0:T(8,128)(2,1)S(1)} %get-tuple-element.17.a_ref), custom_call_target="tpu_custom_call" | custom-call | tf_op jit(solution)/shard_map/group_gather/pallas_call | solution.py:282
  139.7 2.1 dispatch.1
  141.9 1.2 copy-done.2
  143.0 106.0 %experts.1 = bf16[8,48,2048]{2,1,0:T(8,128)(2,1)} custom-call(bf16[8,48,2048]{2,1,0:T(8,128)(2,1)} %bitcast.20, bf16[2048,352]{1,0:T(8,128)(2,1)} %copy.25.wg_ref, bf16[2048,352]{1,0:T(8,128)(2,1)} %copy.26.wu_ref, bf16[352,2048]{1,0:T(8,128)(2,1)} %collective-permute-done.2.wd_ref), custom_call_target="tpu_custom_call" | custom-call | tf_op jit(solution)/shard_map/experts/pallas_call | solution.py:600
  249.0 1.4 copy-done.1
  250.4 1.2 combine.1
  251.7 21.3 %group_scatter.1.part_ref = bf16[8,32,2048]{2,1,0:T(8,128)(2,1)S(1)} custom-call(bf16[8,32,2048]{2,1,0:T(8,128)(2,1)S(1)} %bitcast.19), custom_call_target="tpu_custom_call" | custom-call | tf_op jit(solution)/shard_map/group_scatter/pallas_call | solution.py:282
  273.0 0.8 finish.1
  (29 shorter events, 0.6 us)
Async XLA Ops:
  6.5 92.3 %copy-start.3 = (s32[8192]{0:T(1024)S(1)}, s32[8192]{0:T(1024)}, u32[]{:S(2)}) copy-start(s32[8192]{0:T(1024)} %param.15) | copy-start | bytes 98308
  6.5 21.0 %copy-start.6 = (bf16[512,128]{1,0:T(8,128)(2,1)S(1)}, bf16[512,128]{1,0:T(8,128)(2,1)}, u32[]{:S(2)}) copy-start(bf16[512,128]{1,0:T(8,128)(2,1)} %k_ref.1) | copy-start | bytes 393220
  6.5 21.0 %copy-start.7 = (bf16[512,128]{1,0:T(8,128)(2,1)S(1)}, bf16[512,128]{1,0:T(8,128)(2,1)}, u32[]{:S(2)}) copy-start(bf16[512,128]{1,0:T(8,128)(2,1)} %v_ref.1) | copy-start | bytes 393220
  6.5 92.3 %copy-start.5 = (bf16[512,128]{1,0:T(8,128)(2,1)S(1)}, bf16[512,128]{1,0:T(8,128)(2,1)}, u32[]{:S(2)}) copy-start(bf16[512,128]{1,0:T(8,128)(2,1)} %q_ref.1) | copy-start | bytes 393220
  6.5 109.7 %all-gather.2.cloned.1.call-start = ((), (), s32[]{:S(2)}) async-start(), calls=%async_computation | async-start | bytes 8912896 | tf_op jit(solution)/shard_map/all_gather | solution.py:664
  7.3 104.8 %collective-permute-start = (bf16[2048,352]{0,1:T(8,128)(2,1)}, bf16[2048,352]{0,1:T(8,128)(2,1)}, u32[]{:S(2)}, u32[]{:S(2)}) collective-permute-start(bf16[2048,352]{0,1:T(8,128)(2,1)} %bitcast.26), channel_id=1, source_target_pairs={{0,0},{1,32},{2,2},{3,34},{4,4},{5,36},{6,6},{7,38},{8,8},{9,40},{... | collective-permute-start | bytes 4325384 | tf_op jit(solution)/shard_map/ppermute | solution.py:661
  12.2 102.5 %collective-permute-start.1 = (bf16[2048,352]{0,1:T(8,128)(2,1)}, bf16[2048,352]{0,1:T(8,128)(2,1)S(1)}, u32[]{:S(2)}, u32[]{:S(2)}) collective-permute-start(bf16[2048,352]{0,1:T(8,128)(2,1)} %bitcast.27), channel_id=1, source_target_pairs={{0,0},{1,32},{2,2},{3,34},{4,4},{5,36},{6,6},{7,38},{8,8},{9,40},{... | collective-permute-start | bytes 4325384 | tf_op jit(solution)/shard_map/ppermute | solution.py:662
  14.1 128.9 %collective-permute-start.2 = (bf16[352,2048]{1,0:T(8,128)(2,1)}, bf16[352,2048]{1,0:T(8,128)(2,1)}, u32[]{:S(2)}, u32[]{:S(2)}) collective-permute-start(bf16[352,2048]{1,0:T(8,128)(2,1)} %bitcast.28), channel_id=1, source_target_pairs={{0,0},{1,32},{2,2},{3,34},{4,4},{5,36},{6,6},{7,38},{8,8},{9,40},{... | collective-permute-start | bytes 4325384 | tf_op jit(solution)/shard_map/ppermute | solution.py:663
  114.7 1.6 copy-start.4
  114.7 1.6 copy-start.8
  116.3 3.4 %copy-start = (bf16[2048,2048]{1,0:T(8,128)(2,1)S(1)}, bf16[2048,2048]{1,0:T(8,128)(2,1)}, u32[]{:S(2)}) copy-start(bf16[2048,2048]{1,0:T(8,128)(2,1)} %all-gather.2.cloned.1.call-done.w_ref) | copy-start | bytes 25165828
  141.9 1.2 copy-start.2
  249.0 1.4 copy-start.1
Sparse Core Ops, SparseCore 0:
  10.1 97.5 all-gather.1

commit v2 on v0

v2 whole, which is shorter than its diff:
```python
import jax
import jax.numpy as jnp
from jax import lax
from jax.experimental import pallas as pl
from jax.experimental.pallas import tpu as pltpu
from jax.sharding import PartitionSpec as P

HD = 128
CAP = 6
WINDOW = 2
MESH = pl.DeviceIdType.MESH
ANY = pl.BlockSpec(memory_space=pl.ANY)
BF16 = jnp.bfloat16
F32 = jnp.float32
LOG2E = 1.4426950408889634


def remote(src, dst, send, recv, ctx, ep):
    return pltpu.make_async_remote_copy(
        src_ref=src,
        dst_ref=dst,
        send_sem=send,
        recv_sem=recv,
        device_id=(ctx, ep),
        device_id_type=MESH,
    )


def greet(peers):
    barrier = pltpu.get_barrier_semaphore()
    for ctx, ep in peers:
        pl.semaphore_signal(barrier, inc=1, device_id=(ctx, ep), device_id_type=MESH)
    pl.semaphore_wait(barrier, len(peers))


def params(collective_id, vmem=60 << 20):
    return pltpu.CompilerParams(
        collective_id=collective_id, has_side_effects=True, vmem_limit_bytes=vmem
    )


def device(c, e, dz=0, dy=0, mirror=False):
    z, x, y, x_hi, core = c // 2, c % 2, e // 4, (e // 2) % 2, e % 2
    if mirror:
        x, x_hi = 1 - x, 1 - x_hi
    return ((z + dz + 8) % 8) * 2 + x, ((y + dy + 4) % 4) * 4 + x_hi * 2 + core


GROUP = [(dy, side) for dy in range(4) for side in (False, True)][1:]


def slot_of(dy, side):
    return ((dy + 4) % 4) * 2 + int(side)


def front_kernel(
    q_ref,
    k_ref,
    v_ref,
    seg_ref,
    w_ref,
    res_ref,
    gain_ref,
    route_ref,
    router_ref,
    own_wg,
    own_wu,
    stream_ref,
    rows_ref,
    weight_ref,
    moved_wg,
    moved_wu,
    kv,
    queries,
    away_acc,
    away_stat,
    there_acc,
    there_stat,
    w,
    att,
    heads,
    normed,
    tok_ref,
    routes_ref,
    best,
    total,
    acc,
    kv_send,
    kv_recv,
    w_send,
    w_recv,
    h_send,
    h_recv,
    r_send,
    r_recv,
    t_send,
    t_recv,
    m_send,
    m_recv,
):
    c, e = lax.axis_index("ctx"), lax.axis_index("ep")
    z, x = c // 2, c % 2
    ox = 1 - x
    tok = res_ref.shape[0]
    rows = q_ref.shape[0]
    per = rows // 128
    scale = (HD**-0.5) * LOG2E
    up, down, side = (((z + 1) % 8) * 2 + x, e), (((z + 7) % 8) * 2 + x, e), (z * 2 + ox, e)
    north, south = device(c, e, dy=1), device(c, e, dy=-1)
    across = device(c, e, mirror=True)
    sibling = (c, e + 1 - 2 * (e % 2))
    diagonal = (c + 2 - 4 * (z % 2), e + 1 - 2 * (e % 2))
    everyone = [(c, (e + d) % 16) for d in range(1, 16)]
    everyone += [device(c, e, dy=dy, mirror=True) for dy in range(4)]
    greet(everyone + [up, down, side, diagonal])
    started = []

    def line(send, recv):
        count = [0]

        def go(src, dst, to):
            i = count[0]
            count[0] += 1
            copy = remote(src, dst, send.at[i], recv.at[i], *to)
            copy.start()
            started.append(copy)
            return copy

        return go

    go = line(kv_send, kv_recv)
    go_w = line(w_send, w_recv)
    go_r = line(r_send, r_recv)
    go_t = line(t_send, t_recv)

    kv[z, 0] = k_ref[...]
    kv[z, 1] = v_ref[...]
    ask = go(q_ref, queries.at[1], side)
    ups = {1: go(kv.at[z], kv.at[z], up)}
    downs = {1: go(kv.at[z], kv.at[z], down)}
    queries[0] = q_ref[...]

    w[e] = w_ref[...]
    half = w_ref.shape[0] // 2
    own_up = go_w(w.at[e], w.at[e], north)
    own_down = go_w(w.at[e], w.at[e], south)
    crossing = go_w(w.at[e], w.at[e], across)
    shared = [go_w(w.at[e], w.at[e], sibling)]
    e_across = across[1]

    def at_y(base, dy):
        return ((base // 4 + dy + 4) % 4) * 4 + base % 4

    routes = [
        go_r(route_ref, routes_ref.at[slot_of(-dy, far)], device(c, e, dy=dy, mirror=far))
        for dy, far in GROUP
    ]
    routes_ref[0] = route_ref[...]

    moved = (z % 2) != (e % 2)
    swap = [
        remote(src, dst, m_send.at[i], m_recv.at[i], *diagonal)
        for i, (src, dst) in enumerate(
            ((own_wg, moved_wg), (own_wu, moved_wu))
        )
    ]

    def seg_row(block):
        parts = [seg_ref[pl.ds(block * per + i, 1), :] for i in range(per)]
        return jnp.concatenate(parts, axis=1)

    def column(row):
        return jnp.broadcast_to(row, (8, rows)).T[:, 0:1]

    q_seg = jnp.concatenate([column(seg_row(c)), column(seg_row(side[0]))], axis=0)

    def scores(plane):
        s = lax.dot_general(
            queries[...].reshape(2 * rows, HD),
            kv[plane, 0],
            (((1,), (1,)), ((), ())),
            preferred_element_type=F32,
        )
        return s * scale, q_seg == seg_row(plane * 2 + x)

    def tile(plane, wanted):
        @pl.when(wanted)
        def _():
            s, same = scores(plane)
            s = jnp.where(same, s, -1e30)
            old = best[...]
            new = jnp.maximum(old, jnp.max(s, axis=1, keepdims=True))
            p = jnp.exp2(s - new)
            factor = jnp.exp2(old - new)
            best[...] = new
            total[...] = total[...] * factor + jnp.sum(p, axis=1, keepdims=True)
            acc[...] = acc[...] * factor + jnp.dot(
                p.astype(BF16), kv[plane, 1], preferred_element_type=F32
            )

    ask.wait_recv()
    s, same = scores(z)
    i0 = lax.broadcasted_iota(jnp.int32, s.shape, 0)
    i1 = lax.broadcasted_iota(jnp.int32, s.shape, 1)
    reach = jnp.where(i0 < rows, i0, jnp.where(x == 0, rows, -1))
    s = jnp.where(same & (i1 <= reach), s, -1e30)
    new = jnp.maximum(jnp.max(s, axis=1, keepdims=True), -1e29)
    p = jnp.exp2(s - new)
    best[...] = new
    total[...] = jnp.sum(p, axis=1, keepdims=True)
    acc[...] = jnp.dot(p.astype(BF16), kv[z, 1], preferred_element_type=F32)

    for t in range(1, 5):
        below, above = (z + 8 - t) % 8, (z + t) % 8
        ups[t].wait_recv()
        if t <= 2:
            ups[t + 1] = go(kv.at[below], kv.at[below], up)
        elif t == 3:
            ups[4] = go(kv.at[below, 0], kv.at[below, 0], up)
        downs[t].wait_recv()
        if t <= 2:
            downs[t + 1] = go(kv.at[above], kv.at[above], down)
        elif t == 3:
            downs[4] = go(kv.at[above, 1], kv.at[above, 1], down)

            @pl.when(moved)
            def _():
                for copy in swap:
                    copy.start()

        if t == 2:
            crossing.wait_recv()
            far_up = go_w(w.at[e_across], w.at[e_across], north)
            far_down = go_w(w.at[e_across], w.at[e_across], south)
            shared.append(go_w(w.at[e_across], w.at[e_across], sibling))
        tile(below, z >= t)
        if t <= 3:
            tile(above, z + t >= 8)
        if t == 2 or t == 4:
            base = e if t == 2 else e_across
            (own_up if t == 2 else far_up).wait_recv()
            here = w.at[at_y(base, -1), pl.ds(0, half)]
            second_up = go_w(here, here, north)
            here = w.at[at_y(base, -1)]
            shared.append(go_w(here, here, sibling))
            (own_down if t == 2 else far_down).wait_recv()
            here = w.at[at_y(base, 1), pl.ds(half, half)]
            second_down = go_w(here, here, south)
            here = w.at[at_y(base, 1)]
            shared.append(go_w(here, here, sibling))
            if t == 2:
                seconds = [(second_up, second_down, e)]
            else:
                seconds.append((second_up, second_down, e_across))
        if t == 4:
            away_acc[...] = acc[rows : 2 * rows, :].astype(BF16)
            lane = lax.broadcasted_iota(jnp.int32, (rows, HD), 1)
            stat = jnp.where(
                lane == 0, best[rows : 2 * rows, :], total[rows : 2 * rows, :]
            )
            away_stat[...] = stat.T[0:8, :]
            give_acc = go(away_acc, there_acc, side)
            give_stat = go(away_stat, there_stat, side)
    give_acc.wait_recv()
    give_stat.wait_recv()
    stat = there_stat[...].T
    b0, b1 = best[0:rows, :], stat[:, 0:1]
    new = jnp.maximum(b0, b1)
    f0, f1 = jnp.exp2(b0 - new), jnp.exp2(b1 - new)
    whole = total[0:rows, :] * f0 + stat[:, 1:2] * f1
    att[...] = (
        (acc[0:rows, :] * f0 + there_acc[...].astype(F32) * f1) / whole
    ).astype(BF16)

    def mine(of):
        return pl.ds(pl.multiple_of(of * tok, tok), tok)

    arrivals = []
    for d in range(1, 16):
        to = (e + d) % 16
        copy = remote(att.at[mine(to)], heads.at[e], h_send.at[d], h_recv.at[d], c, to)
        copy.start()
        started.append(copy)
        arrivals.append(copy)
    heads[e] = att[mine(e), :]
    for second_up, second_down, base in seconds:
        second_up.wait_recv()
        second_down.wait_recv()
        here = w.at[at_y(base, 2)]
        shared.append(go_w(here, here, sibling))
    for copy in arrivals:
        copy.wait_recv()
    for copy in shared:
        copy.wait_recv()

    def add_head(h, carry):
        return carry + jnp.dot(heads[h], w[h], preferred_element_type=F32)

    s = lax.fori_loop(0, 16, add_head, res_ref[...].astype(F32))
    stream_ref[...] = s
    mean = jnp.mean(s * s, axis=1, keepdims=True)
    normed[...] = (s * lax.rsqrt(mean + 1e-06) * gain_ref[...]).astype(BF16)

    lower, upper = pl.ds(0, tok // 2), pl.ds(tok // 2, tok // 2)
    crossing = go_t(normed, tok_ref.at[1], across)
    arrive_up = [go_t(normed, tok_ref.at[slot_of(-1, 0)], north)]
    arrive_down = [go_t(normed, tok_ref.at[slot_of(1, 0)], south)]
    tok_ref[0] = normed[...]
    crossing.wait_recv()
    arrive_up.append(go_t(tok_ref.at[1], tok_ref.at[slot_of(-1, 1)], north))
    arrive_down.append(go_t(tok_ref.at[1], tok_ref.at[slot_of(1, 1)], south))
    last = []
    for far in (0, 1):
        arrive_up[far].wait_recv()
        here, there = tok_ref.at[slot_of(-1, far)], tok_ref.at[slot_of(2, far)]
        last.append(go_t(here.at[lower], there.at[lower], north))
        arrive_down[far].wait_recv()
        here = tok_ref.at[slot_of(1, far)]
        last.append(go_t(here.at[upper], there.at[upper], south))
    for copy in last + routes:
        copy.wait_recv()
    tokens = tok_ref[...].reshape(8 * tok, tok_ref.shape[2])
    chosen, weights = placement(
        z,
        8 * (e // 2),
        routes_ref[...].reshape(8 * tok, 128),
        router_ref.shape[0],
        tokens,
        router_ref[...],
    )
    rows_ref[...] = lax.dot_general(
        jnp.where(chosen, 1.0, 0.0).astype(BF16),
        tokens,
        (((0,), (0,)), ((), ())),
        preferred_element_type=F32,
    ).astype(BF16)
    weight_ref[...] = weights
    for copy in started:
        copy.wait_send()

    @pl.when(moved)
    def _():
        for copy in swap:
            copy.wait()


def front(
    queries, keys, values, segments, out_weight, residual, gain, routes, router, own
):
    rows = queries.shape[0]
    tok, width = residual.shape
    slots = 64 * CAP
    vmem = pl.BlockSpec(memory_space=pltpu.VMEM)
    dma = pltpu.SemaphoreType.DMA
    return pl.pallas_call(
        front_kernel,
        out_shape=(
            jax.ShapeDtypeStruct((tok, width), F32),
            jax.ShapeDtypeStruct((slots, width), BF16),
            jax.ShapeDtypeStruct((8 * tok, slots), F32),
            *[jax.ShapeDtypeStruct(w.shape, w.dtype) for w in own],
        ),
        in_specs=[vmem] * 9 + [ANY] * 2,
        out_specs=(vmem, vmem, vmem, ANY, ANY),
        scratch_shapes=[
            pltpu.VMEM((8, 2, rows, HD), BF16),
            pltpu.VMEM((2, rows, HD), BF16),
            pltpu.VMEM((rows, HD), BF16),
            pltpu.VMEM((8, rows), F32),
            pltpu.VMEM((rows, HD), BF16),
            pltpu.VMEM((8, rows), F32),
            pltpu.VMEM((16,) + out_weight.shape, BF16),
            pltpu.VMEM((rows, HD), BF16),
            pltpu.VMEM((16, tok, HD), BF16),
            pltpu.VMEM((tok, width), BF16),
            pltpu.VMEM((8, tok, width), BF16),
            pltpu.VMEM((8,) + routes.shape, jnp.int32),
            pltpu.VMEM((2 * rows, 1), F32),
            pltpu.VMEM((2 * rows, 1), F32),
            pltpu.VMEM((2 * rows, HD), F32),
            dma((11,)),
            dma((11,)),
            dma((18,)),
            dma((18,)),
            dma((16,)),
            dma((16,)),
            dma((7,)),
            dma((7,)),
            dma((9,)),
            dma((9,)),
            dma((2,)),
            dma((2,)),
        ],
        compiler_params=params(1),
        name="front",
    )(
        queries,
        keys,
        values,
        segments.reshape(-1, 128),
        out_weight,
        residual,
        gain.reshape(1, width),
        routes,
        router,
        *own,
    )


def placement(z, first, routes, experts, tokens, router):
    count = routes.shape[0]
    slots = 8 * CAP
    width = 8 * slots
    ids = lax.broadcasted_iota(jnp.int32, (count, experts), 1)
    named = routes[:, 0:1] == ids
    for k in range(1, 6):
        named = named | (routes[:, k : k + 1] == ids)
    named = jnp.where(named, 1.0, 0.0)
    t0 = lax.broadcasted_iota(jnp.int32, (count, count), 0)
    t1 = lax.broadcasted_iota(jnp.int32, (count, count), 1)
    before = jnp.where((t1 < t0) & ((t1 >> 5) == (t0 >> 5)), 1.0, 0.0).astype(BF16)
    rank = jnp.dot(before, named.astype(BF16), preferred_element_type=F32)
    owner = lax.broadcasted_iota(jnp.int32, (count, experts), 0) >> 5
    place = jnp.where(named > 0, rank + (owner * CAP).astype(F32), -1.0)
    col = lax.broadcasted_iota(jnp.int32, (experts, width), 1)
    block = jnp.zeros_like(col)
    for k in range(1, 8):
        block = block + jnp.where(col >= k * slots, 1, 0)
    at = (z + 8 - ((block + 1) >> 1) * (2 * (block & 1) - 1)) & 7
    expert = first + 4 * (at & 1) + (at >> 1)
    pick = jnp.where(
        lax.broadcasted_iota(jnp.int32, (experts, width), 0) == expert, 1.0, 0.0
    ).astype(BF16)
    spread = jnp.dot(place.astype(BF16), pick, preferred_element_type=F32)
    chosen = spread == (col[0:1, :] - slots * block[0:1, :]).astype(F32)
    high = router.astype(BF16)
    low = (router - high.astype(F32)).astype(BF16)
    dims = (((1,), (1,)), ((), ()))
    logits = lax.dot_general(
        tokens, high, dims, preferred_element_type=F32
    ) + lax.dot_general(tokens, low, dims, preferred_element_type=F32)
    gates = named * jax.nn.sigmoid(logits)
    weights = gates / jnp.sum(gates, axis=1, keepdims=True)
    high = weights.astype(BF16)
    low = (weights - high.astype(F32)).astype(BF16)
    spread = jnp.dot(high, pick, preferred_element_type=F32) + jnp.dot(
        low, pick, preferred_element_type=F32
    )
    return chosen, jnp.where(chosen, spread, 0.0)


def combine_kernel(weight_ref, rows_ref, out_ref):
    weights = weight_ref[...]
    high = weights.astype(BF16)
    low = (weights - high.astype(F32)).astype(BF16)
    rows = rows_ref[...]
    out_ref[...] = (
        jnp.dot(high, rows, preferred_element_type=F32)
        + jnp.dot(low, rows, preferred_element_type=F32)
    ).astype(BF16)


def combine(weights, rows):
    return pl.pallas_call(
        combine_kernel,
        out_shape=jax.ShapeDtypeStruct((weights.shape[0], rows.shape[1]), BF16),
        compiler_params=pltpu.CompilerParams(vmem_limit_bytes=32 << 20),
        name="combine",
    )(weights, rows)


def final_kernel(stream_ref, part_ref, out_ref):
    total = stream_ref[...]
    for m in range(8):
        total = total + part_ref[m].astype(F32)
    out_ref[...] = total.astype(BF16)


def finish(stream, parts):
    return pl.pallas_call(
        final_kernel,
        out_shape=jax.ShapeDtypeStruct(stream.shape, BF16),
        compiler_params=pltpu.CompilerParams(vmem_limit_bytes=32 << 20),
        name="finish",
    )(stream, parts)


def scatter_kernel(a_ref, a_out, send, recv, local):
    c, e = lax.axis_index("ctx"), lax.axis_index("ep")
    group = [
        (device(c, e, dy=dy, mirror=side), slot_of(dy, side), slot_of(-dy, side))
        for dy, side in GROUP
    ]
    greet([to for to, _, _ in group])
    own = pltpu.make_async_copy(a_ref.at[0], a_out.at[0], local)
    own.start()
    copies = []
    for to, src, dst in group:
        copies.append(remote(a_ref.at[src], a_out.at[dst], send.at[dst], recv.at[dst], *to))
        copies[-1].start()
    for copy in copies:
        copy.wait()
    own.wait()


def group_scatter(rows):
    return pl.pallas_call(
        scatter_kernel,
        out_shape=jax.ShapeDtypeStruct(rows.shape, rows.dtype),
        in_specs=[ANY],
        out_specs=ANY,
        scratch_shapes=[
            pltpu.SemaphoreType.DMA((8,)),
            pltpu.SemaphoreType.DMA((8,)),
            pltpu.SemaphoreType.DMA,
        ],
        compiler_params=params(5),
        name="group_scatter",
    )(rows)


def away(i):
    half = (i + 1) // 2
    return half * (2 * (i % 2) - 1)


def expert_kernel(
    rows_ref,
    own_wg,
    own_wu,
    own_wd,
    moved_wg,
    moved_wu,
    back_ref,
    xs,
    ps,
    from_core,
    from_side,
    sums,
    done,
    wg,
    wu,
    wd,
    z_send,
    z_recv,
    x_send,
    x_recv,
    s_send,
    s_recv,
    c_send,
    c_recv,
    f_send,
    f_recv,
    b_send,
    b_recv,
    w_send,
    w_recv,
    local,
):
    c, e = lax.axis_index("ctx"), lax.axis_index("ep")
    z, x = c // 2, c % 2
    side, other = z * 2 + (1 - x), e + 1 - 2 * (e % 2)
    n = 8
    moved = (z % 2) != (e % 2)
    diagonal = (c + 2 - 4 * (z % 2), other)
    swap = remote(own_wd, wd, w_send, w_recv, *diagonal)

    def load(refs):
        copies = []
        for i, (src, dst) in enumerate(zip(refs, (wg, wu, wd))):
            copies.append(pltpu.make_async_copy(src, dst, local.at[i]))
        return copies

    @pl.when(moved)
    def _():
        for copy in load((moved_wg, moved_wu)):
            copy.start()

    @pl.when(jnp.logical_not(moved))
    def _():
        for copy in load((own_wg, own_wu, own_wd)):
            copy.start()

    own = pltpu.make_async_copy(rows_ref.at[0], xs.at[0, 0], local.at[3])
    own.start()
    peers = [(((z + d) % n) * 2 + x, e) for d in range(1, n)]
    greet(peers + [(side, e), (c, other), diagonal])

    def out(i):
        to = ((z + n - away(i)) % n) * 2 + x
        return remote(rows_ref.at[i], xs.at[i, 0], z_send.at[i], z_recv.at[i], to, e)

    def to_side(i):
        return remote(xs.at[i, 0], xs.at[i, 1], x_send.at[i], x_recv.at[i], side, e)

    def to_core(i, q):
        return remote(
            xs.at[i, q], xs.at[i, q + 2], s_send.at[i, q], s_recv.at[i, q], c, other
        )

    def sum_core(i):
        return remote(
            ps.at[i, pl.ds(2, 2)], from_core.at[i], c_send.at[i], c_recv.at[i], c, other
        )

    def sum_side(i):
        return remote(
            sums.at[i], from_side.at[i], f_send.at[i], f_recv.at[i], side, e
        )

    def home(i):
        to = ((z + n + away(i)) % n) * 2 + x
        return remote(done.at[i], back_ref.at[i], b_send.at[i], b_recv.at[i], to, e)

    for i in range(1, WINDOW + 1):
        out(i).start()

    @pl.when(moved)
    def _():
        swap.start()

    own.wait()
    for copy in load((own_wg, own_wu)):
        copy.wait()

    def step(s, carry):
        @pl.when(s < n)
        def _():
            @pl.when(s > 0)
            def _():
                out(s).wait_recv()

            @pl.when((s > 0) & (s + WINDOW < n))
            def _():
                out(s + WINDOW).start()

            to_side(s).start()
            to_core(s, 0).start()

        @pl.when((s >= 1) & (s < n + 1))
        def _():
            i = s - 1
            to_side(i).wait_recv()
            to_core(i, 1).start()

        @pl.when((s >= 2) & (s < n + 2))
        def _():
            i = s - 2

            @pl.when((s == 2) & moved)
            def _():
                swap.wait_recv()

            @pl.when((s == 2) & jnp.logical_not(moved))
            def _():
                pltpu.make_async_copy(own_wd, wd, local.at[2]).wait()

            to_core(i, 0).wait_recv()
            to_core(i, 1).wait_recv()
            shape = xs.shape[1:]
            rows = xs[i].reshape(shape[0] * shape[1], shape[2])
            dims = (((1,), (1,)), ((), ()))
            gate = lax.dot_general(rows, wg[...], dims, preferred_element_type=F32)
            upper = lax.dot_general(rows, wu[...], dims, preferred_element_type=F32)
            act = (gate / (1.0 + jnp.exp(-gate)) * upper).astype(BF16)
            part = jnp.dot(act, wd[...], preferred_element_type=F32)
            ps[i] = part.astype(BF16).reshape(shape)
            sum_core(i).start()

        @pl.when((s >= 3) & (s < n + 3))
        def _():
            i = s - 3
            sum_core(i).wait_recv()
            sums[i] = (ps[i, 1].astype(F32) + from_core[i, 1].astype(F32)).astype(BF16)
            sum_side(i).start()

        @pl.when(s >= 4)
        def _():
            i = s - 4
            sum_side(i).wait_recv()
            done[i] = (
                ps[i, 0].astype(F32) + from_core[i, 0].astype(F32) + from_side[i].astype(F32)
            ).astype(BF16)

            @pl.when(i > 0)
            def _():
                home(i).start()

        return carry

    lax.fori_loop(0, n + 4, step, 0)
    last = pltpu.make_async_copy(done.at[0], back_ref.at[0], local.at[3])
    last.start()

    def drain(i, carry):
        to_side(i).wait_send()
        to_core(i, 0).wait_send()
        to_core(i, 1).wait_send()
        sum_core(i).wait_send()
        sum_side(i).wait_send()

        @pl.when(i > 0)
        def _():
            out(i).wait_send()
            home(i).wait()

        return carry

    lax.fori_loop(0, n, drain, 0)

    @pl.when(moved)
    def _():
        swap.wait_send()

    last.wait()


def experts(rows, own, moved):
    wg, wu, wd = own
    n, cap, width = rows.shape
    dma = pltpu.SemaphoreType.DMA
    return pl.pallas_call(
        expert_kernel,
        out_shape=jax.ShapeDtypeStruct(rows.shape, BF16),
        in_specs=[ANY] * 6,
        out_specs=ANY,
        scratch_shapes=[
            pltpu.VMEM((n, 4, cap, width), BF16),
            pltpu.VMEM((n, 4, cap, width), BF16),
            pltpu.VMEM((n, 2, cap, width), BF16),
            pltpu.VMEM((n, cap, width), BF16),
            pltpu.VMEM((n, cap, width), BF16),
            pltpu.VMEM((n, cap, width), BF16),
            pltpu.VMEM(wg.shape, BF16),
            pltpu.VMEM(wu.shape, BF16),
            pltpu.VMEM(wd.shape, BF16),
            dma((n,)),
            dma((n,)),
            dma((n,)),
            dma((n,)),
            dma((n, 2)),
            dma((n, 2)),
            dma((n,)),
            dma((n,)),
            dma((n,)),
            dma((n,)),
            dma((n,)),
            dma((n,)),
            dma,
            dma,
            dma((4,)),
        ],
        compiler_params=params(3),
        name="experts",
    )(rows, *own, *moved)


def body(
    queries,
    keys,
    values,
    segments,
    residual,
    out_weight,
    norm_gain,
    router,
    routes,
    gate_weight,
    up_weight,
    down_weight,
):
    tok, width = residual.shape
    own = (gate_weight[0, 0].T, up_weight[0, 0].T, down_weight[0, 0])
    padded = jnp.pad(routes, ((0, 0), (0, 128 - routes.shape[1])), constant_values=-1)
    stream, rows, weights, *moved = front(
        queries,
        keys,
        values,
        segments,
        out_weight,
        residual,
        norm_gain,
        padded,
        router.T,
        own[:2],
    )
    slots = 8 * CAP
    back = experts(rows.reshape(8, slots, width), own, moved)
    mixed = combine(weights, back.reshape(8 * slots, width))
    parts = group_scatter(mixed.reshape(8, tok, width))
    return finish(stream, parts)


def solution(mesh):
    placed = (
        P("ctx", "ep"),
        P("ctx", "ep"),
        P("ctx", "ep"),
        P(),
        P(("ctx", "ep"), None),
        P("ep", None),
        P(),
        P(),
        P(("ctx", "ep"), None),
        P("ep", "ctx", None, None),
        P("ep", "ctx", None, None),
        P("ep", "ctx", None, None),
    )
    return jax.shard_map(
        body, mesh=mesh, in_specs=placed, out_specs=P(("ctx", "ep"), None), check_vma=False
    )
```

time: 627 us -> 213 us (0.34)
  blocking collectives: 315 us -> 0 us
  Pallas kernels: 0 us -> 204 us
  waiting for transfers between devices: 127 us -> 0 us
  matrix products: 70.8 us -> 0 us
  local copies, waits for them, and re-layouts: 70.8 us -> 5.02 us
  starting transfers between devices: 16 us -> 0 us
  between operations: 13.6 us -> 0.08 us
  other arithmetic: 11.2 us -> 0 us
    all_to_all x3 -> x0, blocking collectives: 315 us -> none  [the longest x1 146 us: body(): lax.all_to_all(copies, 'ctx', split_axis=0, concat_axis=0, tiled=True)]
    pallas_call x0 -> x5, Pallas kernels: none -> 204 us  [the longest x1 110 us: experts(): pl.pallas_call(expert_kernel, out_shape=jax.ShapeDtypeStruct(rows.shape,...]
    all_gather x2 -> x0, waiting for transfers between devices: 98.5 us -> none  [the longest x1 98.1 us: in_one_piece(): whole, at, done = (lax.all_gather(both, axis, axis=dim, tiled=True), 0, [])]
    dot_general x38 -> x0, matrix products: 70.8 us -> none  [the longest x16 22.3 us: one_block(): jnp.einsum('hqk,khd->qhd', expo.astype(jnp.bfloat16), value_block, prefer...]
    reshape x6 -> x0, local copies, waits for them, and re-layouts: 34.9 us -> none  [the longest x2 18.5 us: body(): partial_value = jnp.dot(act, down_local, preferred_element_type=jnp.float...]
    all_to_all x2 -> x0, waiting for transfers between devices: 27.4 us -> none  [the longest x1 19.9 us: body(): lax.all_to_all(jnp.swapaxes(summed, 0, 1), 'ep', split_axis=0, concat_axi...]
    all_to_all x2 -> x0, starting transfers between devices: 16 us -> none  [the longest x1 8.86 us: body(): lax.all_to_all(attended, 'ep', split_axis=0, concat_axis=1, tiled=True)]
    dynamic_slice x17 -> x0, local copies, waits for them, and re-layouts: 13.1 us -> none  [the longest x16 12.3 us: one_block(): k_seg = lax.dynamic_slice_in_dim(segments, offset, width)]
  transfers between devices with their start and end apart: 4 -> 0, of which waited for: 4 -> 0; matrix products, arithmetic and copies ran while one was open for 12% -> 0% of each run, Pallas kernels for 0% -> 0%
where the time goes in v2:
time: 213 us; the launch traced here: 209 us
  Pallas kernels  204 us (96%)
  local copies, waits for them, and re-layouts  5.02 us (2%)
    pallas_call x1, Pallas kernels, experts(): pl.pallas_call(expert_kernel, out_shape=jax.ShapeDtypeStruct(rows.shape,...  110 us
    pallas_call x1, Pallas kernels, front(): pl.pallas_call(front_kernel, out_shape=(jax.ShapeDtypeStruct((tok, width)...  74.7 us
    pallas_call x1, Pallas kernels, group_scatter(): pl.pallas_call(scatter_kernel, out_shape=jax.ShapeDtypeStruct(rows.shape,...  16.8 us
    unnamed x11, local copies, waits for them, and re-layouts  4.41 us

profile of v2, /device:TPU:1, one launch (start us, length us, event | category | flops | bytes accessed | tf_op | source)
XLA Modules:
  0.0 208.8 jit_solution(12681801460113305281)
XLA Ops:
  0.0 0.8 copy.13
  0.8 0.6 pad.4.route_ref
  1.4 74.7 %front.1 = (f32[32,2048]{1,0:T(8,128)}, bf16[384,2048]{1,0:T(8,128)(2,1)}, f32[256,384]{1,0:T(8,128)}, bf16[352,2048]{1,0:T(8,128)(2,1)}, bf16[352,2048]{1,0:T(8,128)(2,1)}) custom-call(bf16[512,128]{1,0:T(8,128)(2,1)} %q_ref.1, bf16[512,128]{1,0:T(8,128)(2,1)} %k_ref.1, bf16[512,128]{1,0:T(8,128)(2,1)} %v_ref.1, s32[64,128]{1,0:T(8,128)} %bitcast.22, ...), custom_call_target="tpu_custom_call" | custom-call | tf_op jit(solution)/shard_map/front/pallas_call | solution.py:355
  76.1 0.0 copy-start.3
  76.1 110.2 %experts.1 = bf16[8,48,2048]{2,1,0:T(8,128)(2,1)} custom-call(bf16[8,48,2048]{2,1,0:T(8,128)(2,1)} %bitcast.19, bf16[352,2048]{1,0:T(8,128)(2,1)} %bitcast.16, bf16[352,2048]{1,0:T(8,128)(2,1)} %bitcast.18, bf16[352,2048]{1,0:T(8,128)(2,1)} %bitcast.20, bf16[352,2048]{1,0:T(8,128)(2,1)} %get-tuple-element.13.moved_wg, ...), custom_call_target="tpu_custom_call" | custom-call | tf_op jit(solution)/shard_map/experts/pallas_call | solution.py:722
  186.2 0.0 copy-done.3
  186.2 0.0 copy-start
  186.3 1.4 copy-done
  187.7 1.2 combine.1
  188.9 0.0 copy-start.1
  188.9 1.0 copy-done.1
  189.9 0.0 copy-start.4
  189.9 16.8 %group_scatter.1.part_ref = bf16[8,32,2048]{2,1,0:T(8,128)(2,1)} custom-call(bf16[8,32,2048]{2,1,0:T(8,128)(2,1)} %bitcast.14), custom_call_target="tpu_custom_call" | custom-call | tf_op jit(solution)/shard_map/group_scatter/pallas_call | solution.py:507
  206.7 0.0 copy-done.4
  206.8 0.0 copy-start.2
  206.8 1.2 copy-done.2
  208.0 0.8 finish.1
Async XLA Ops:
  76.1 110.2 %copy-start.3 = (f32[256,384]{1,0:T(8,128)S(1)}, f32[256,384]{1,0:T(8,128)}, u32[]{:S(2)}) copy-start(f32[256,384]{1,0:T(8,128)} %get-tuple-element.11.weight_ref) | copy-start | bytes 1179652
  186.2 1.4 copy-start
  188.9 1.0 copy-start.1
  189.9 16.8 %copy-start.4 = (f32[32,2048]{1,0:T(8,128)S(1)}, f32[32,2048]{1,0:T(8,128)}, u32[]{:S(2)}) copy-start(f32[32,2048]{1,0:T(8,128)} %get-tuple-element.10.stream_ref) | copy-start | bytes 786436
  206.8 1.2 copy-start.2

commit v3 on v2

--- a/solution.py
+++ b/solution.py
@@ -65,11 +65,13 @@
     router_ref,
     own_wg,
     own_wu,
+    own_wd,
     stream_ref,
     rows_ref,
     weight_ref,
     moved_wg,
     moved_wu,
+    moved_wd,
     kv,
     queries,
     away_acc,
@@ -135,6 +137,7 @@
 
     kv[z, 0] = k_ref[...]
     kv[z, 1] = v_ref[...]
+    away_stat[...] = jnp.zeros_like(away_stat)
     ask = go(q_ref, queries.at[1], side)
     ups = {1: go(kv.at[z], kv.at[z], up)}
     downs = {1: go(kv.at[z], kv.at[z], down)}
@@ -158,57 +161,71 @@
     routes_ref[0] = route_ref[...]
 
     moved = (z % 2) != (e % 2)
-    swap = [
-        remote(src, dst, m_send.at[i], m_recv.at[i], *diagonal)
-        for i, (src, dst) in enumerate(
-            ((own_wg, moved_wg), (own_wu, moved_wu))
-        )
-    ]
+    halves = own_wg.shape[0] // 2
+    swap = []
+    for src, dst in ((own_wg, moved_wg), (own_wu, moved_wu), (own_wd, moved_wd)):
+        for at in (pl.ds(0, halves), pl.ds(halves, halves)):
+            i = len(swap)
+            swap.append(
+                remote(src.at[at], dst.at[at], m_send.at[i], m_recv.at[i], *diagonal)
+            )
+
+    def push(*pieces):
+        @pl.when(moved)
+        def _():
+            for i in pieces:
+                swap[i].start()
 
     def seg_row(block):
         parts = [seg_ref[pl.ds(block * per + i, 1), :] for i in range(per)]
         return jnp.concatenate(parts, axis=1)
 
-    def column(row):
-        return jnp.broadcast_to(row, (8, rows)).T[:, 0:1]
-
-    q_seg = jnp.concatenate([column(seg_row(c)), column(seg_row(side[0]))], axis=0)
+    ids = jnp.concatenate([seg_row(c), seg_row(side[0])], axis=1)
+    below_1 = jnp.sum(jnp.where(seg_ref[...] < 1, 1, 0), keepdims=True)
+    below_2 = jnp.sum(jnp.where(seg_ref[...] < 2, 1, 0), keepdims=True)
+    start = jnp.where(ids < 1, 0, jnp.where(ids < 2, below_1, below_2))
 
     def scores(plane):
         s = lax.dot_general(
+            kv[plane, 0],
             queries[...].reshape(2 * rows, HD),
-            kv[plane, 0],
             (((1,), (1,)), ((), ())),
             preferred_element_type=F32,
         )
-        return s * scale, q_seg == seg_row(plane * 2 + x)
+        key = lax.broadcasted_iota(jnp.int32, s.shape, 0)
+        return s, key, key >= start - (plane * 2 + x) * rows
+
+    def mix(plane, p):
+        return lax.dot_general(
+            kv[plane, 1],
+            p.astype(BF16),
+            (((0,), (0,)), ((), ())),
+            preferred_element_type=F32,
+        )
 
     def tile(plane, wanted):
         @pl.when(wanted)
         def _():
-            s, same = scores(plane)
+            s, _, same = scores(plane)
             s = jnp.where(same, s, -1e30)
             old = best[...]
-            new = jnp.maximum(old, jnp.max(s, axis=1, keepdims=True))
-            p = jnp.exp2(s - new)
-            factor = jnp.exp2(old - new)
+            new = jnp.maximum(old, jnp.max(s, axis=0, keepdims=True))
+            p = jnp.exp2((s - new) * scale)
+            factor = jnp.exp2((old - new) * scale)
             best[...] = new
-            total[...] = total[...] * factor + jnp.sum(p, axis=1, keepdims=True)
-            acc[...] = acc[...] * factor + jnp.dot(
-                p.astype(BF16), kv[plane, 1], preferred_element_type=F32
-            )
+            total[...] = total[...] * factor + jnp.sum(p, axis=0, keepdims=True)
+            acc[...] = acc[...] * factor + mix(plane, p)
 
     ask.wait_recv()
-    s, same = scores(z)
-    i0 = lax.broadcasted_iota(jnp.int32, s.shape, 0)
-    i1 = lax.broadcasted_iota(jnp.int32, s.shape, 1)
-    reach = jnp.where(i0 < rows, i0, jnp.where(x == 0, rows, -1))
-    s = jnp.where(same & (i1 <= reach), s, -1e30)
-    new = jnp.maximum(jnp.max(s, axis=1, keepdims=True), -1e29)
-    p = jnp.exp2(s - new)
+    s, key, same = scores(z)
+    lane = lax.broadcasted_iota(jnp.int32, (1, 2 * rows), 1)
+    reach = jnp.where(lane < rows, lane, jnp.where(x == 0, rows, -1))
+    s = jnp.where(same & (key <= reach), s, -1e30)
+    new = jnp.maximum(jnp.max(s, axis=0, keepdims=True), -1e29)
+    p = jnp.exp2((s - new) * scale)
     best[...] = new
-    total[...] = jnp.sum(p, axis=1, keepdims=True)
-    acc[...] = jnp.dot(p.astype(BF16), kv[z, 1], preferred_element_type=F32)
+    total[...] = jnp.sum(p, axis=0, keepdims=True)
+    acc[...] = mix(z, p)
 
     for t in range(1, 5):
         below, above = (z + 8 - t) % 8, (z + t) % 8
@@ -223,12 +240,10 @@
         elif t == 3:
             downs[4] = go(kv.at[above, 1], kv.at[above, 1], down)
 
-            @pl.when(moved)
-            def _():
-                for copy in swap:
-                    copy.start()
+            push(1, 2)
 
         if t == 2:
+            push(0)
             crossing.wait_recv()
             far_up = go_w(w.at[e_across], w.at[e_across], north)
             far_down = go_w(w.at[e_across], w.at[e_across], south)
@@ -253,24 +268,19 @@
             else:
                 seconds.append((second_up, second_down, e_across))
         if t == 4:
-            away_acc[...] = acc[rows : 2 * rows, :].astype(BF16)
-            lane = lax.broadcasted_iota(jnp.int32, (rows, HD), 1)
-            stat = jnp.where(
-                lane == 0, best[rows : 2 * rows, :], total[rows : 2 * rows, :]
-            )
-            away_stat[...] = stat.T[0:8, :]
+            away_acc[...] = acc[:, rows : 2 * rows].astype(BF16)
+            away_stat[0:1, :] = best[:, rows : 2 * rows]
+            away_stat[1:2, :] = total[:, rows : 2 * rows]
             give_acc = go(away_acc, there_acc, side)
             give_stat = go(away_stat, there_stat, side)
     give_acc.wait_recv()
     give_stat.wait_recv()
-    stat = there_stat[...].T
-    b0, b1 = best[0:rows, :], stat[:, 0:1]
+    b0, b1 = best[:, 0:rows], there_stat[0:1, :]
     new = jnp.maximum(b0, b1)
-    f0, f1 = jnp.exp2(b0 - new), jnp.exp2(b1 - new)
-    whole = total[0:rows, :] * f0 + stat[:, 1:2] * f1
-    att[...] = (
-        (acc[0:rows, :] * f0 + there_acc[...].astype(F32) * f1) / whole
-    ).astype(BF16)
+    f0, f1 = jnp.exp2((b0 - new) * scale), jnp.exp2((b1 - new) * scale)
+    whole = total[:, 0:rows] * f0 + there_stat[1:2, :] * f1
+    mixed = (acc[:, 0:rows] * f0 + there_acc[...].astype(F32) * f1) / whole
+    att[...] = mixed.T.astype(BF16)
 
     def mine(of):
         return pl.ds(pl.multiple_of(of * tok, tok), tok)
@@ -283,6 +293,7 @@
         started.append(copy)
         arrivals.append(copy)
     heads[e] = att[mine(e), :]
+    push(3)
     for second_up, second_down, base in seconds:
         second_up.wait_recv()
         second_down.wait_recv()
@@ -293,10 +304,11 @@
     for copy in shared:
         copy.wait_recv()
 
-    def add_head(h, carry):
-        return carry + jnp.dot(heads[h], w[h], preferred_element_type=F32)
-
-    s = lax.fori_loop(0, 16, add_head, res_ref[...].astype(F32))
+    push(4)
+    wide = jnp.concatenate([heads[h] for h in range(16)], axis=1)
+    s = res_ref[...].astype(F32) + jnp.dot(
+        wide, w[...].reshape(wide.shape[1], -1), preferred_element_type=F32
+    )
     stream_ref[...] = s
     mean = jnp.mean(s * s, axis=1, keepdims=True)
     normed[...] = (s * lax.rsqrt(mean + 1e-06) * gain_ref[...]).astype(BF16)
@@ -306,6 +318,7 @@
     arrive_up = [go_t(normed, tok_ref.at[slot_of(-1, 0)], north)]
     arrive_down = [go_t(normed, tok_ref.at[slot_of(1, 0)], south)]
     tok_ref[0] = normed[...]
+    push(5)
     crossing.wait_recv()
     arrive_up.append(go_t(tok_ref.at[1], tok_ref.at[slot_of(-1, 1)], north))
     arrive_down.append(go_t(tok_ref.at[1], tok_ref.at[slot_of(1, 1)], south))
@@ -360,14 +373,14 @@
             jax.ShapeDtypeStruct((8 * tok, slots), F32),
             *[jax.ShapeDtypeStruct(w.shape, w.dtype) for w in own],
         ),
-        in_specs=[vmem] * 9 + [ANY] * 2,
-        out_specs=(vmem, vmem, vmem, ANY, ANY),
+        in_specs=[vmem] * 9 + [ANY] * 3,
+        out_specs=(vmem, vmem, vmem, ANY, ANY, ANY),
         scratch_shapes=[
             pltpu.VMEM((8, 2, rows, HD), BF16),
             pltpu.VMEM((2, rows, HD), BF16),
-            pltpu.VMEM((rows, HD), BF16),
+            pltpu.VMEM((HD, rows), BF16),
             pltpu.VMEM((8, rows), F32),
-            pltpu.VMEM((rows, HD), BF16),
+            pltpu.VMEM((HD, rows), BF16),
             pltpu.VMEM((8, rows), F32),
             pltpu.VMEM((16,) + out_weight.shape, BF16),
             pltpu.VMEM((rows, HD), BF16),
@@ -375,9 +388,9 @@
             pltpu.VMEM((tok, width), BF16),
             pltpu.VMEM((8, tok, width), BF16),
             pltpu.VMEM((8,) + routes.shape, jnp.int32),
-            pltpu.VMEM((2 * rows, 1), F32),
-            pltpu.VMEM((2 * rows, 1), F32),
-            pltpu.VMEM((2 * rows, HD), F32),
+            pltpu.VMEM((1, 2 * rows), F32),
+            pltpu.VMEM((1, 2 * rows), F32),
+            pltpu.VMEM((HD, 2 * rows), F32),
             dma((11,)),
             dma((11,)),
             dma((18,)),
@@ -388,8 +401,8 @@
             dma((7,)),
             dma((9,)),
             dma((9,)),
-            dma((2,)),
-            dma((2,)),
+            dma((6,)),
+            dma((6,)),
         ],
         compiler_params=params(1),
         name="front",
@@ -426,7 +439,8 @@
     block = jnp.zeros_like(col)
     for k in range(1, 8):
         block = block + jnp.where(col >= k * slots, 1, 0)
-    at = (z + 8 - ((block + 1) >> 1) * (2 * (block & 1) - 1)) & 7
+    turn = (8 - block) & 7
+    at = (z + 8 - ((turn + 1) >> 1) * (2 * (turn & 1) - 1)) & 7
     expert = first + 4 * (at & 1) + (at >> 1)
     pick = jnp.where(
         lax.broadcasted_iota(jnp.int32, (experts, width), 0) == expert, 1.0, 0.0
@@ -449,77 +463,8 @@
     return chosen, jnp.where(chosen, spread, 0.0)
 
 
-def combine_kernel(weight_ref, rows_ref, out_ref):
-    weights = weight_ref[...]
-    high = weights.astype(BF16)
-    low = (weights - high.astype(F32)).astype(BF16)
-    rows = rows_ref[...]
-    out_ref[...] = (
-        jnp.dot(high, rows, preferred_element_type=F32)
-        + jnp.dot(low, rows, preferred_element_type=F32)
-    ).astype(BF16)
-
-
-def combine(weights, rows):
-    return pl.pallas_call(
-        combine_kernel,
-        out_shape=jax.ShapeDtypeStruct((weights.shape[0], rows.shape[1]), BF16),
-        compiler_params=pltpu.CompilerParams(vmem_limit_bytes=32 << 20),
-        name="combine",
-    )(weights, rows)
-
-
-def final_kernel(stream_ref, part_ref, out_ref):
-    total = stream_ref[...]
-    for m in range(8):
-        total = total + part_ref[m].astype(F32)
-    out_ref[...] = total.astype(BF16)
-
-
-def finish(stream, parts):
-    return pl.pallas_call(
-        final_kernel,
-        out_shape=jax.ShapeDtypeStruct(stream.shape, BF16),
-        compiler_params=pltpu.CompilerParams(vmem_limit_bytes=32 << 20),
-        name="finish",
-    )(stream, parts)
-
-
-def scatter_kernel(a_ref, a_out, send, recv, local):
-    c, e = lax.axis_index("ctx"), lax.axis_index("ep")
-    group = [
-        (device(c, e, dy=dy, mirror=side), slot_of(dy, side), slot_of(-dy, side))
-        for dy, side in GROUP
-    ]
-    greet([to for to, _, _ in group])
-    own = pltpu.make_async_copy(a_ref.at[0], a_out.at[0], local)
-    own.start()
-    copies = []
-    for to, src, dst in group:
-        copies.append(remote(a_ref.at[src], a_out.at[dst], send.at[dst], recv.at[dst], *to))
-        copies[-1].start()
-    for copy in copies:
-        copy.wait()
-    own.wait()
-
-
-def group_scatter(rows):
-    return pl.pallas_call(
-        scatter_kernel,
-        out_shape=jax.ShapeDtypeStruct(rows.shape, rows.dtype),
-        in_specs=[ANY],
-        out_specs=ANY,
-        scratch_shapes=[
-            pltpu.SemaphoreType.DMA((8,)),
-            pltpu.SemaphoreType.DMA((8,)),
-            pltpu.SemaphoreType.DMA,
-        ],
-        compiler_params=params(5),
-        name="group_scatter",
-    )(rows)
-
-
 def away(i):
+    i = (8 - i) % 8
     half = (i + 1) // 2
     return half * (2 * (i % 2) - 1)
 
@@ -531,7 +476,13 @@
     own_wd,
     moved_wg,
     moved_wu,
+    moved_wd,
+    weight_ref,
+    stream_ref,
+    out_ref,
     back_ref,
+    parts,
+    got,
     xs,
     ps,
     from_core,
@@ -553,8 +504,8 @@
     f_recv,
     b_send,
     b_recv,
-    w_send,
-    w_recv,
+    p_send,
+    p_recv,
     local,
 ):
     c, e = lax.axis_index("ctx"), lax.axis_index("ep")
@@ -562,8 +513,6 @@
     side, other = z * 2 + (1 - x), e + 1 - 2 * (e % 2)
     n = 8
     moved = (z % 2) != (e % 2)
-    diagonal = (c + 2 - 4 * (z % 2), other)
-    swap = remote(own_wd, wd, w_send, w_recv, *diagonal)
 
     def load(refs):
         copies = []
@@ -573,7 +522,7 @@
 
     @pl.when(moved)
     def _():
-        for copy in load((moved_wg, moved_wu)):
+        for copy in load((moved_wg, moved_wu, moved_wd)):
             copy.start()
 
     @pl.when(jnp.logical_not(moved))
@@ -584,7 +533,11 @@
     own = pltpu.make_async_copy(rows_ref.at[0], xs.at[0, 0], local.at[3])
     own.start()
     peers = [(((z + d) % n) * 2 + x, e) for d in range(1, n)]
-    greet(peers + [(side, e), (c, other), diagonal])
+    group = [
+        (device(c, e, dy=dy, mirror=far), slot_of(dy, far), slot_of(-dy, far))
+        for dy, far in GROUP
+    ]
+    greet(peers + [(side, e), (c, other)] + [to for to, _, _ in group])
 
     def out(i):
         to = ((z + n - away(i)) % n) * 2 + x
@@ -615,12 +568,8 @@
     for i in range(1, WINDOW + 1):
         out(i).start()
 
-    @pl.when(moved)
-    def _():
-        swap.start()
-
     own.wait()
-    for copy in load((own_wg, own_wu)):
+    for copy in load((own_wg, own_wu, own_wd)):
         copy.wait()
 
     def step(s, carry):
@@ -643,17 +592,28 @@
             to_side(i).wait_recv()
             to_core(i, 1).start()
 
+        @pl.when((s >= 3) & (s < n + 3))
+        def _():
+            i = s - 3
+            sum_core(i).wait_recv()
+            sums[i] = (ps[i, 1].astype(F32) + from_core[i, 1].astype(F32)).astype(BF16)
+            sum_side(i).start()
+
+        @pl.when(s >= 4)
+        def _():
+            i = s - 4
+            sum_side(i).wait_recv()
+            done[i] = (
+                ps[i, 0].astype(F32) + from_core[i, 0].astype(F32) + from_side[i].astype(F32)
+            ).astype(BF16)
+
+            @pl.when(i > 0)
+            def _():
+                home(i).start()
+
         @pl.when((s >= 2) & (s < n + 2))
         def _():
             i = s - 2
-
-            @pl.when((s == 2) & moved)
-            def _():
-                swap.wait_recv()
-
-            @pl.when((s == 2) & jnp.logical_not(moved))
-            def _():
-                pltpu.make_async_copy(own_wd, wd, local.at[2]).wait()
 
             to_core(i, 0).wait_recv()
             to_core(i, 1).wait_recv()
@@ -667,30 +627,31 @@
             ps[i] = part.astype(BF16).reshape(shape)
             sum_core(i).start()
 
-        @pl.when((s >= 3) & (s < n + 3))
-        def _():
-            i = s - 3
-            sum_core(i).wait_recv()
-            sums[i] = (ps[i, 1].astype(F32) + from_core[i, 1].astype(F32)).astype(BF16)
-            sum_side(i).start()
-
-        @pl.when(s >= 4)
-        def _():
-            i = s - 4
-            sum_side(i).wait_recv()
-            done[i] = (
-                ps[i, 0].astype(F32) + from_core[i, 0].astype(F32) + from_side[i].astype(F32)
-            ).astype(BF16)
-
-            @pl.when(i > 0)
-            def _():
-                home(i).start()
-
         return carry
 
     lax.fori_loop(0, n + 4, step, 0)
-    last = pltpu.make_async_copy(done.at[0], back_ref.at[0], local.at[3])
-    last.start()
+    back_ref[0] = done[0]
+
+    def arrive(i, carry):
+        home(i).wait_recv()
+        return carry
+
+    lax.fori_loop(1, n, arrive, 0)
+    weights = weight_ref[...]
+    high = weights.astype(BF16)
+    low = (weights - high.astype(F32)).astype(BF16)
+    rows = back_ref[...].reshape(-1, back_ref.shape[2])
+    mixed = jnp.dot(high, rows, preferred_element_type=F32) + jnp.dot(
+        low, rows, preferred_element_type=F32
+    )
+    parts[...] = mixed.astype(BF16).reshape(parts.shape)
+    copies = []
+    for to, src, dst in group:
+        copies.append(
+            remote(parts.at[src], got.at[dst], p_send.at[dst], p_recv.at[dst], *to)
+        )
+        copies[-1].start()
+    total = stream_ref[...] + parts[0].astype(F32)
 
     def drain(i, carry):
         to_side(i).wait_send()
@@ -702,29 +663,33 @@
         @pl.when(i > 0)
         def _():
             out(i).wait_send()
-            home(i).wait()
+            home(i).wait_send()
 
         return carry
 
     lax.fori_loop(0, n, drain, 0)
-
-    @pl.when(moved)
-    def _():
-        swap.wait_send()
-
-    last.wait()
-
-
-def experts(rows, own, moved):
+    for copy in copies:
+        copy.wait_recv()
+    for m in range(1, 8):
+        total = total + got[m].astype(F32)
+    out_ref[...] = total.astype(BF16)
+    for copy in copies:
+        copy.wait_send()
+
+
+def experts(rows, own, moved, weights, stream):
     wg, wu, wd = own
     n, cap, width = rows.shape
     dma = pltpu.SemaphoreType.DMA
     return pl.pallas_call(
         expert_kernel,
-        out_shape=jax.ShapeDtypeStruct(rows.shape, BF16),
-        in_specs=[ANY] * 6,
-        out_specs=ANY,
+        out_shape=jax.ShapeDtypeStruct(stream.shape, BF16),
+        in_specs=[ANY] * 7 + [pl.BlockSpec(memory_space=pltpu.VMEM)] * 2,
+        out_specs=pl.BlockSpec(memory_space=pltpu.VMEM),
         scratch_shapes=[
+            pltpu.VMEM((n, cap, width), BF16),
+            pltpu.VMEM((8,) + stream.shape, BF16),
+            pltpu.VMEM((8,) + stream.shape, BF16),
             pltpu.VMEM((n, 4, cap, width), BF16),
             pltpu.VMEM((n, 4, cap, width), BF16),
             pltpu.VMEM((n, 2, cap, width), BF16),
@@ -746,13 +711,13 @@
             dma((n,)),
             dma((n,)),
             dma((n,)),
-            dma,
-            dma,
+            dma((8,)),
+            dma((8,)),
             dma((4,)),
         ],
         compiler_params=params(3),
         name="experts",
-    )(rows, *own, *moved)
+    )(rows, *own, *moved, weights, stream)
 
 
 def body(
@@ -782,13 +747,9 @@
         norm_gain,
         padded,
         router.T,
-        own[:2],
-    )
-    slots = 8 * CAP
-    back = experts(rows.reshape(8, slots, width), own, moved)
-    mixed = combine(weights, back.reshape(8 * slots, width))
-    parts = group_scatter(mixed.reshape(8, tok, width))
-    return finish(stream, parts)
+        own,
+    )
+    return experts(rows.reshape(8, 8 * CAP, width), own, moved, weights, stream)
 
 
 def solution(mesh):

time: 213 us -> 200 us (0.939); the launches traced: 209 us -> 200 us
  Pallas kernels: 204 us -> 197 us
    pallas_call x4 -> x1, Pallas kernels: 129 us -> 111 us  [experts(): pl.pallas_call(expert_kernel, out_shape=jax.ShapeDtypeStruct(stream.shape...]
    pallas_call x1, Pallas kernels: 74.7 us -> 85.9 us  [front(): pl.pallas_call(front_kernel, out_shape=(jax.ShapeDtypeStruct((tok, width)...]
    unnamed x11 -> x2, local copies, waits for them, and re-layouts: 4.41 us -> 2.34 us
where the time goes in v3:
time: 200 us
  Pallas kernels  197 us (98%)
  local copies, waits for them, and re-layouts  2.95 us (1%)
    pallas_call x1, Pallas kernels, experts(): pl.pallas_call(expert_kernel, out_shape=jax.ShapeDtypeStruct(stream.shape...  111 us
    pallas_call x1, Pallas kernels, front(): pl.pallas_call(front_kernel, out_shape=(jax.ShapeDtypeStruct((tok, width)...  85.9 us

profile of v3, /device:TPU:1, one launch (start us, length us, event | category | flops | bytes accessed | tf_op | source)
XLA Modules:
  0.0 200.1 jit_solution(9773021787452893118)
XLA Ops:
  0.0 0.8 copy.13
  0.8 0.6 pad.4.route_ref
  1.4 85.9 %front.1 = (f32[32,2048]{1,0:T(8,128)}, bf16[384,2048]{1,0:T(8,128)(2,1)}, f32[256,384]{1,0:T(8,128)}, bf16[352,2048]{1,0:T(8,128)(2,1)}, bf16[352,2048]{1,0:T(8,128)(2,1)}, /*index=5*/bf16[352,2048]{1,0:T(8,128)(2,1)}) custom-call(bf16[512,128]{1,0:T(8,128)(2,1)} %q_ref.1, bf16[512,128]{1,0:T(8,128)(2,1)} %k_ref.1, bf16[512,128]{1,0:T(8,128)(2,1)} %v_ref.1, ...), custom_call_target="tpu_custom_call" | custom-call | tf_op jit(solution)/shard_map/front/pallas_call | solution.py:368
  87.3 111.2 %experts.1 = bf16[32,2048]{1,0:T(8,128)(2,1)} custom-call(bf16[8,48,2048]{2,1,0:T(8,128)(2,1)} %bitcast.17, bf16[352,2048]{1,0:T(8,128)(2,1)} %bitcast.12, bf16[352,2048]{1,0:T(8,128)(2,1)} %bitcast.14, bf16[352,2048]{1,0:T(8,128)(2,1)} %bitcast.16, bf16[352,2048]{1,0:T(8,128)(2,1)} %get-tuple-element.12.moved_wg, ...), custom_call_target="tpu_custom_call" | custom-call | tf_op jit(solution)/shard_map/experts/pallas_call | solution.py:684
  198.6 1.6 copy.15

commit v4 on v3

--- a/solution.py
+++ b/solution.py
@@ -240,10 +240,11 @@
         elif t == 3:
             downs[4] = go(kv.at[above, 1], kv.at[above, 1], down)
 
-            push(1, 2)
-
+            push(2, 3)
+
+        if t <= 2:
+            push(t - 1)
         if t == 2:
-            push(0)
             crossing.wait_recv()
             far_up = go_w(w.at[e_across], w.at[e_across], north)
             far_down = go_w(w.at[e_across], w.at[e_across], south)
@@ -293,7 +294,7 @@
         started.append(copy)
         arrivals.append(copy)
     heads[e] = att[mine(e), :]
-    push(3)
+    push(4)
     for second_up, second_down, base in seconds:
         second_up.wait_recv()
         second_down.wait_recv()
@@ -304,7 +305,7 @@
     for copy in shared:
         copy.wait_recv()
 
-    push(4)
+    push(5)
     wide = jnp.concatenate([heads[h] for h in range(16)], axis=1)
     s = res_ref[...].astype(F32) + jnp.dot(
         wide, w[...].reshape(wide.shape[1], -1), preferred_element_type=F32
@@ -318,7 +319,6 @@
     arrive_up = [go_t(normed, tok_ref.at[slot_of(-1, 0)], north)]
     arrive_down = [go_t(normed, tok_ref.at[slot_of(1, 0)], south)]
     tok_ref[0] = normed[...]
-    push(5)
     crossing.wait_recv()
     arrive_up.append(go_t(tok_ref.at[1], tok_ref.at[slot_of(-1, 1)], north))
     arrive_down.append(go_t(tok_ref.at[1], tok_ref.at[slot_of(1, 1)], south))

time: 200 us -> 200 us (level); the launches traced: 200 us -> 197 us
  Pallas kernels: 197 us -> 194 us
    pallas_call x1, Pallas kernels: 85.9 us -> 83.9 us  [front(): pl.pallas_call(front_kernel, out_shape=(jax.ShapeDtypeStruct((tok, width)...]
where the time goes in v4:
time: 200 us; the launch traced here: 197 us
  Pallas kernels  194 us (97%)
  local copies, waits for them, and re-layouts  2.95 us (1%)
    pallas_call x1, Pallas kernels, experts(): pl.pallas_call(expert_kernel, out_shape=jax.ShapeDtypeStruct(stream.shape...  110 us
    pallas_call x1, Pallas kernels, front(): pl.pallas_call(front_kernel, out_shape=(jax.ShapeDtypeStruct((tok, width)...  83.9 us

profile of v4, /device:TPU:1, one launch (start us, length us, event | category | flops | bytes accessed | tf_op | source)
XLA Modules:
  0.0 196.7 jit_solution(6401647540590869800)
XLA Ops:
  0.0 0.8 copy.13
  0.8 0.6 pad.4.route_ref
  1.4 83.9 %front.1 = (f32[32,2048]{1,0:T(8,128)}, bf16[384,2048]{1,0:T(8,128)(2,1)}, f32[256,384]{1,0:T(8,128)}, bf16[352,2048]{1,0:T(8,128)(2,1)}, bf16[352,2048]{1,0:T(8,128)(2,1)}, /*index=5*/bf16[352,2048]{1,0:T(8,128)(2,1)}) custom-call(bf16[512,128]{1,0:T(8,128)(2,1)} %q_ref.1, bf16[512,128]{1,0:T(8,128)(2,1)} %k_ref.1, bf16[512,128]{1,0:T(8,128)(2,1)} %v_ref.1, ...), custom_call_target="tpu_custom_call" | custom-call | tf_op jit(solution)/shard_map/front/pallas_call | solution.py:368
  85.2 109.9 %experts.1 = bf16[32,2048]{1,0:T(8,128)(2,1)} custom-call(bf16[8,48,2048]{2,1,0:T(8,128)(2,1)} %bitcast.17, bf16[352,2048]{1,0:T(8,128)(2,1)} %bitcast.12, bf16[352,2048]{1,0:T(8,128)(2,1)} %bitcast.14, bf16[352,2048]{1,0:T(8,128)(2,1)} %bitcast.16, bf16[352,2048]{1,0:T(8,128)(2,1)} %get-tuple-element.12.moved_wg, ...), custom_call_target="tpu_custom_call" | custom-call | tf_op jit(solution)/shard_map/experts/pallas_call | solution.py:684
  195.1 1.6 copy.15
